TPU v7x, 32 devices: a whole 2x2x4 slice. The times are simulated.
32 devices in a mesh: dp: 8 (over z, y), tensor: 4 (over x, core).
Axes of the slice: x: 2, y: 2, z: 4, core: 2. Of those that a mesh axis runs over, the one named last changes fastest.
Arguments:
- tokens: bfloat16 [16384, 768], P(('dp', 'tensor')), may hold values from -6 to 6
- query_weight: bfloat16 [768, 768], P('dp', 'tensor'), may hold values from -0.21875 to 0.21875
- w_key: bfloat16 [768, 768], P('dp', 'tensor'), may hold values from -0.21875 to 0.21875
- value_weight: bfloat16 [768, 768], P('dp', 'tensor'), may hold values from -0.21875 to 0.21875
- w_out: bfloat16 [768, 768], P('tensor', 'dp'), may hold values from -0.875 to 0.875
- w_in: bfloat16 [768, 3072], P('dp', 'tensor'), may hold values from -0.21875 to 0.21875
- w_down: bfloat16 [3072, 768], P('tensor', 'dp'), may hold values from -0.109375 to 0.109375
- gain_attn: float32 [768], replicated, may hold values from 0.5 to 1.5
- shift_attn: float32 [768], replicated, may hold values from -0.6 to 0.6
- gain_ffn: float32 [768], replicated, may hold values from 0.5 to 1.5
- shift_ffn: float32 [768], replicated, may hold values from -0.6 to 0.6
- query_down_factor: bfloat16 [768, 8], replicated, may hold values from -0.21875 to 0.21875
- query_up_factor: bfloat16 [8, 768], P(None, 'tensor'), may hold values from -1 to 1
- value_down_factor: bfloat16 [768, 8], replicated, may hold values from -0.21875 to 0.21875
- value_up_factor: bfloat16 [8, 768], P(None, 'tensor'), may hold values from -1 to 1
- lengths: int32 [8, 32], P('dp'), may hold values from 0 to 512, as said below
- cotangent: bfloat16 [16384, 768], P(('dp', 'tensor')), may hold values from -6 to 6
Outputs:
- mixed: bfloat16 [16384, 768], P(('dp', 'tensor'))
- grad_tokens: bfloat16 [16384, 768], P(('dp', 'tensor'))
- grad_a_query: float32 [768, 8], replicated
- query_up_gradient: float32 [8, 768], P(None, 'tensor')
- grad_a_value: float32 [768, 8], replicated
- value_up_gradient: float32 [8, 768], P(None, 'tensor')
Inputs may be any that keep to these rules, and one draw needn't show every extreme that they name: `lengths`: row g lists the sequences of data group g, laid end to end from the group's first position; they cover at most 2048 positions and the rest is padding; 0 marks an empty slot; some group holds a document of 512 tokens.
All inputs are finite; a program needn't handle non-finite values.
Results may differ from a plain program's by a relative error of at most 0.019.
Values may be sent and summed in bfloat16 or wider, within the bound.
A program may use at most 128 MiB of HBM per device.

v0:
```python
import functools
import heapq

import jax
import jax.numpy as jnp
from jax import lax
from jax.experimental import pallas as pl
from jax.experimental.pallas import tpu as pltpu
from jax.sharding import PartitionSpec as P

HEAD_DIM = 64
PAIR = 2 * HEAD_DIM
Q_BLOCK = 256
K_BLOCK = 512
FFN_BLOCK = 256
FORWARD_GROUP = 3
BACKWARD_GROUP = 3
ADAPTER_SCALE = 2.0
SCORE_SCALE = HEAD_DIM ** (-0.5)
LOG2_SCALE = SCORE_SCALE * 1.4426950408889634
NEG_FILL = -1e30
LN_EPS = 1e-05
VMEM_LIMIT = 56 * 1024 * 1024


def dot_nn(left, right):
    return jnp.dot(left, right, preferred_element_type=jnp.float32)


def dot_nt(left, right):
    return lax.dot_general(
        left, right, (((1,), (1,)), ((), ())), preferred_element_type=jnp.float32
    )


def dot_tn(left, right):
    return lax.dot_general(
        left, right, (((0,), (0,)), ((), ())), preferred_element_type=jnp.float32
    )


def norm_forward(row_vals, gain_vals, offset):
    middle = jnp.mean(row_vals, axis=-1, keepdims=True)
    centred = row_vals - middle
    inverse = lax.rsqrt(jnp.mean(centred * centred, axis=-1, keepdims=True) + LN_EPS)
    normed = centred * inverse
    return (normed * gain_vals + offset, normed, inverse)


def norm_backward(grad_out, normed, inverse, gain_vals):
    grad_n = grad_out * gain_vals
    return inverse * (
        grad_n
        - jnp.mean(grad_n, axis=-1, keepdims=True)
        - normed * jnp.mean(grad_n * normed, axis=-1, keepdims=True)
    )


def gelu_parts(hidden):
    cdf_part = 0.5 * (1.0 + lax.erf(hidden * 0.7071067811865476))
    density = jnp.exp(-0.5 * hidden * hidden) * 0.3989422804014327
    return (hidden * cdf_part, cdf_part + hidden * density)


def block_span(lengths_ref, first_row, rows, total_rows):
    last_row = first_row + rows - 1

    def slot_step(slot, carry):
        end, low, high = carry
        end = end + lengths_ref[0, slot]
        low = jnp.where(end <= first_row, jnp.maximum(low, end), low)
        high = jnp.where(end > last_row, jnp.minimum(high, end), high)
        return end, low, high

    start = (jnp.int32(0), jnp.int32(0), jnp.int32(total_rows))
    _, low, high = lax.fori_loop(0, lengths_ref.shape[1], slot_step, start, unroll=8)
    return low, high


def row_bounds(lengths_ref, first_row, rows, total_rows):
    place = first_row + lax.broadcasted_iota(jnp.int32, (1, rows), 1)

    def slot_step(slot, carry):
        end, begin, finish = carry
        end = end + lengths_ref[0, slot]
        done = place >= end
        begin = jnp.where(done, jnp.maximum(begin, end), begin)
        finish = jnp.where(done, finish, jnp.minimum(finish, end))
        return end, begin, finish

    start = (
        jnp.int32(0),
        jnp.zeros((1, rows), jnp.int32),
        jnp.full((1, rows), total_rows, jnp.int32),
    )
    _, begin, finish = lax.fori_loop(0, lengths_ref.shape[1], slot_step, start, unroll=8)
    return begin, finish


def stack_pair(block):
    lane = lax.broadcasted_iota(jnp.int32, block.shape, 1)
    zero = jnp.zeros_like(block)
    return jnp.concatenate(
        [jnp.where(lane < HEAD_DIM, block, zero), jnp.where(lane >= HEAD_DIM, block, zero)],
        axis=0,
    )


def unstack_pair(block, rows):
    joined = jnp.concatenate([block[:HEAD_DIM, :rows], block[HEAD_DIM:, rows:]], axis=0)
    return joined.T


def window_mask(step, low, begin, finish, total_rows):
    wanted = low + step * K_BLOCK
    start = pl.multiple_of(jnp.minimum(wanted, total_rows - K_BLOCK), 16)
    key_at = start + lax.broadcasted_iota(jnp.int32, (K_BLOCK, begin.shape[1]), 0)
    return start, (key_at >= jnp.maximum(begin, wanted)) & (key_at < finish)


def each_q_block(lengths_ref, rows, total_rows, group, heads_width, block_step):
    base = lax.axis_index("tensor") * rows

    @pl.loop(0, rows // Q_BLOCK)
    def _(q_at):
        first_row = base + q_at * Q_BLOCK
        low, high = block_span(lengths_ref, first_row, Q_BLOCK, total_rows)
        low = (low // 16) * 16
        steps = (high - low + K_BLOCK - 1) // K_BLOCK
        begin, finish = row_bounds(lengths_ref, first_row, Q_BLOCK, total_rows)
        q_rows = pl.ds(pl.multiple_of(q_at * Q_BLOCK, Q_BLOCK), Q_BLOCK)

        @pl.loop(0, heads_width // PAIR // group)
        def _(at):
            pairs = [at * group + i for i in range(group)]
            lanes = [pl.ds(pl.multiple_of(pair * PAIR, PAIR), PAIR) for pair in pairs]
            slots = [q_at * (heads_width // PAIR) + pair for pair in pairs]
            block_step(q_rows, lanes, slots, low, steps, begin, finish)


def forward_kernel(lengths_ref, q_ref, k_ref, v_ref, out_ref, lse_ref):
    total_rows = k_ref.shape[0]

    def block_step(q_rows, lanes, slots, low, steps, begin, finish):
        q_two = [stack_pair(q_ref[q_rows, lane]) for lane in lanes]

        def body(step, carry):
            start, allowed = window_mask(step, low, begin, finish, total_rows)
            window = pl.ds(start, K_BLOCK)
            both = jnp.concatenate([allowed, allowed], axis=1)
            result = []
            for (top, total, acc), q_pair, lane in zip(carry, q_two, lanes):
                scores = jnp.where(both, dot_nt(k_ref[window, lane], q_pair), NEG_FILL)
                new_top = jnp.maximum(top, jnp.max(scores, axis=0, keepdims=True))
                probs = jnp.exp2((scores - new_top) * LOG2_SCALE)
                shrink = jnp.exp2((top - new_top) * LOG2_SCALE)
                total = total * shrink + jnp.sum(probs, axis=0, keepdims=True)
                acc = acc * shrink + dot_tn(v_ref[window, lane], probs.astype(jnp.bfloat16))
                result.append((new_top, total, acc))
            return tuple(result)

        empty = (
            jnp.full((1, 2 * Q_BLOCK), NEG_FILL, jnp.float32),
            jnp.zeros((1, 2 * Q_BLOCK), jnp.float32),
            jnp.zeros((PAIR, 2 * Q_BLOCK), jnp.float32),
        )
        final = lax.fori_loop(0, steps, body, (empty,) * len(lanes))
        for (top, total, acc), lane, slot in zip(final, lanes, slots):
            out_ref[q_rows, lane] = unstack_pair(acc / total, Q_BLOCK).astype(jnp.bfloat16)
            lse_ref[slot] = top * LOG2_SCALE + jnp.log2(total)

    each_q_block(
        lengths_ref, q_ref.shape[0], total_rows, FORWARD_GROUP, q_ref.shape[1], block_step
    )


def backward_kernel(
    lengths_ref,
    q_ref,
    k_ref,
    v_ref,
    ctx_ref,
    lse_ref,
    grad_ref,
    gq_ref,
    gk_ref,
    gv_ref,
    gk_acc,
    gv_acc,
):
    total_rows = k_ref.shape[0]
    gk_acc[...] = jnp.zeros_like(gk_acc)
    gv_acc[...] = jnp.zeros_like(gv_acc)

    def block_step(q_rows, lanes, slots, low, steps, begin, finish):
        ready = []
        for lane, slot in zip(lanes, slots):
            grads = grad_ref[q_rows, lane]
            product = (grads.astype(jnp.float32) * ctx_ref[q_rows, lane].astype(jnp.float32)).T
            row_dot = jnp.concatenate(
                [
                    jnp.sum(product[:HEAD_DIM], axis=0, keepdims=True),
                    jnp.sum(product[HEAD_DIM:], axis=0, keepdims=True),
                ],
                axis=1,
            )
            ready.append((stack_pair(q_ref[q_rows, lane]), stack_pair(grads), row_dot, lse_ref[slot]))

        def body(step, carry):
            start, allowed = window_mask(step, low, begin, finish, total_rows)
            window = pl.ds(start, K_BLOCK)
            both = jnp.concatenate([allowed, allowed], axis=1)
            result = []
            for acc, (q_pair, grad_pair, row_dot, lse), lane in zip(carry, ready, lanes):
                keys = k_ref[window, lane]
                scores = jnp.where(both, dot_nt(keys, q_pair), NEG_FILL)
                probs = jnp.exp2(scores * LOG2_SCALE - lse)
                grad_probs = dot_nt(v_ref[window, lane], grad_pair)
                grad_scores = (probs * (grad_probs - row_dot)).astype(jnp.bfloat16)
                gk_acc[window, lane] += dot_nn(grad_scores, q_pair)
                gv_acc[window, lane] += dot_nn(probs.astype(jnp.bfloat16), grad_pair)
                result.append(acc + dot_tn(keys, grad_scores))
            return tuple(result)

        zero = jnp.zeros((PAIR, 2 * Q_BLOCK), jnp.float32)
        final = lax.fori_loop(0, steps, body, (zero,) * len(lanes))
        for acc, lane in zip(final, lanes):
            gq_ref[q_rows, lane] = (unstack_pair(acc, Q_BLOCK) * SCORE_SCALE).astype(jnp.bfloat16)

    each_q_block(
        lengths_ref, q_ref.shape[0], total_rows, BACKWARD_GROUP, q_ref.shape[1], block_step
    )

    @pl.loop(0, total_rows // K_BLOCK)
    def _(at):
        window = pl.ds(pl.multiple_of(at * K_BLOCK, K_BLOCK), K_BLOCK)
        gk_ref[window, :] = (gk_acc[window, :] * SCORE_SCALE).astype(jnp.bfloat16)
        gv_ref[window, :] = gv_acc[window, :].astype(jnp.bfloat16)


VMEM_SPEC = pl.BlockSpec(memory_space=pltpu.VMEM)
HBM_SPEC = pl.BlockSpec(memory_space=pltpu.HBM)
SMEM_SPEC = pl.BlockSpec(memory_space=pltpu.SMEM)


def attend_forward(lengths, q_own, k_all, v_all):
    rows, width = q_own.shape
    heads = width // HEAD_DIM
    return pl.pallas_call(
        forward_kernel,
        out_shape=(
            jax.ShapeDtypeStruct((rows, width), jnp.bfloat16),
            jax.ShapeDtypeStruct((rows // Q_BLOCK * heads // 2, 1, 2 * Q_BLOCK), jnp.float32),
        ),
        in_specs=[SMEM_SPEC] + [VMEM_SPEC] * 3,
        out_specs=(VMEM_SPEC, VMEM_SPEC),
        compiler_params=pltpu.CompilerParams(vmem_limit_bytes=VMEM_LIMIT),
        name="attend_forward",
    )(lengths, q_own, k_all, v_all)


def attend_backward(lengths, q_own, k_all, v_all, context, lse, grad_context):
    rows, width = q_own.shape
    total_rows = k_all.shape[0]
    return pl.pallas_call(
        backward_kernel,
        out_shape=(
            jax.ShapeDtypeStruct((rows, width), jnp.bfloat16),
            jax.ShapeDtypeStruct((total_rows, width), jnp.bfloat16),
            jax.ShapeDtypeStruct((total_rows, width), jnp.bfloat16),
        ),
        in_specs=[SMEM_SPEC] + [VMEM_SPEC] * 6,
        out_specs=(VMEM_SPEC,) * 3,
        scratch_shapes=[
            pltpu.VMEM((total_rows, width), jnp.float32),
            pltpu.VMEM((total_rows, width), jnp.float32),
        ],
        compiler_params=pltpu.CompilerParams(vmem_limit_bytes=VMEM_LIMIT),
        name="attend_backward",
    )(lengths, q_own, k_all, v_all, context, lse, grad_context)


MESH_ID = pl.DeviceIdType.MESH
DEPTH = 4
FULL_ROWS = 96

FLOWS = (
    (0, 0, "zxy", 0.0),
    (0, 1, "zyx", 0.0),
    (1, 0, "xzy", 12.0),
    (1, 1, "zyx", 24.0),
    (2, 0, "xzy", 12.0),
    (2, 1, "yxz", 12.0),
)
OWN = (0, 0, 0)


def forwards(order, piece):
    used = [axis for axis in order if piece["xyz".index(axis)] != 0]
    at = order.index(used[-1]) if used else -1
    steps = []
    if used and used[-1] == "z":
        steps.append(("z", 1 if piece[2] < 0 else -1))
    for axis in order[at + 1 :]:
        steps += [("z", 1), ("z", -1)] if axis == "z" else [(axis, 1)]
    return steps


def passed(piece, axis, sign):
    x, y, z = piece
    if axis == "x":
        return (1 - x, y, z)
    return (x, 1 - y, z) if axis == "y" else (x, y, z - sign)


def event_order(token_time):
    per_piece = 1.7
    links, heap, times, count = {}, [], {}, 0
    for z in range(DEPTH):
        links[z, "x", 1] = token_time
        for flow, (_, _, _, start) in enumerate(FLOWS):
            heapq.heappush(heap, (start + 0.01 * flow, count, z, flow, OWN))
            count += 1
    while heap:
        now, _, z, flow, piece = heapq.heappop(heap)
        times.setdefault((flow, piece), []).append(now)
        for axis, sign in forwards(FLOWS[flow][2], piece):
            there = z + sign if axis == "z" else z
            if not 0 <= there < DEPTH:
                continue
            end = max(links.get((z, axis, sign), 0.0), now) + per_piece
            links[z, axis, sign] = end
            heapq.heappush(heap, (end + 3.0, count, there, flow, passed(piece, axis, sign)))
            count += 1
    return [key for _, key in sorted((sum(v) / len(v), key) for key, v in times.items())]


class Place:
    def __init__(self):
        dp, tensor = lax.axis_index("dp"), lax.axis_index("tensor")
        self.z, self.y = dp // 2, lax.rem(dp, 2)
        self.x, self.core = tensor // 2, lax.rem(tensor, 2)

    def device(self, x=None, y=None, z=None, core=None):
        x = self.x if x is None else x
        y = self.y if y is None else y
        z = self.z if z is None else z
        core = self.core if core is None else core
        return (z * 2 + y, x * 2 + core)

    def step(self, axis, sign):
        if axis == "x":
            return self.device(x=1 - self.x)
        return self.device(y=1 - self.y) if axis == "y" else self.device(z=self.z + sign)

    def sibling(self):
        return self.device(core=1 - self.core)


def gather_kernel(
    wq_ref,
    wk_ref,
    wv_ref,
    wo_ref,
    w_in_ref,
    w_down_ref,
    tokens_ref,
    up_q_ref,
    up_v_ref,
    down_q_ref,
    down_v_ref,
    full_ref,
    weights_hbm,
    rows_hbm,
    q_hbm,
    k_hbm,
    v_hbm,
    ups_full,
    pack_ref,
    packs_ref,
    rows_ref,
    ups_ref,
    ups_all_ref,
    weights_ref,
    q_ref,
    k_ref,
    v_ref,
    piece_recv,
    send_sem,
    sib_send,
    sib_recv,
    own_sem,
    rows_send,
    rows_recv,
    ups_send,
    ups_recv,
    out_sem,
):
    place = Place()
    x, y, z, core = place.x, place.y, place.z, place.core
    token_rows = tokens_ref.shape[0]
    part_rows = FULL_ROWS // 2
    half_rows = token_rows // 2

    barrier = pltpu.get_barrier_semaphore()
    others = (
        place.sibling(),
        place.step("x", 1),
        place.device(x=1 - x, core=1 - core),
        place.step("y", 1),
    )
    for target in others:
        pl.semaphore_signal(barrier, inc=1, device_id=target, device_id_type=MESH_ID)
    for sign, there in ((1, z < DEPTH - 1), (-1, z > 0)):

        @pl.when(there)
        def _(sign=sign):
            pl.semaphore_signal(
                barrier, inc=1, device_id=place.step("z", sign), device_id_type=MESH_ID
            )

    slim = wq_ref.shape[1]
    for kind, ref in enumerate((wq_ref, wk_ref, wv_ref)):
        pack_ref[:, kind * slim : (kind + 1) * slim] = ref[...]
    pack_ref[:, 3 * slim : 4 * slim] = wo_ref[...].astype(jnp.float32).T.astype(jnp.bfloat16)
    ups_ref[...] = jnp.zeros_like(ups_ref)
    ups_ref[0:8, :slim] = up_q_ref[...].astype(jnp.float32)
    ups_ref[8:16, :slim] = up_v_ref[...].astype(jnp.float32)
    shards = (pack_ref, w_in_ref, w_down_ref)
    inner = ((z > 0) & (z < DEPTH - 1)).astype(jnp.int32)
    pl.semaphore_wait(barrier, len(others) + 1 + inner)

    def remote(source, target, send, recv, device):
        return pltpu.make_async_remote_copy(
            src_ref=source,
            dst_ref=target,
            send_sem=send,
            recv_sem=recv,
            device_id=device,
            device_id_type=MESH_ID,
        )

    def rows_at(owner_x, owner_core, half):
        return rows_ref.at[owner_x * 2 + owner_core, pl.ds(half * half_rows, half_rows)]

    own_copies = [
        pltpu.make_async_copy(pack_ref, packs_ref.at[core, x, z, y], own_sem.at[0]),
        pltpu.make_async_copy(tokens_ref, rows_ref.at[x * 2 + core], own_sem.at[1]),
        pltpu.make_async_copy(ups_ref, ups_all_ref.at[x * 2 + core], own_sem.at[2]),
        pltpu.make_async_copy(w_in_ref, full_ref.at[0, core, x, z, y], own_sem.at[3]),
        pltpu.make_async_copy(w_down_ref, full_ref.at[1, core, x, z, y], own_sem.at[4]),
    ]
    row_copies = []
    for half in range(2):
        source = tokens_ref.at[pl.ds(half * half_rows, half_rows)]
        for slot, device in ((0, place.step("x", 1)), (1, place.sibling())):
            row_copies.append(
                remote(
                    source,
                    rows_at(x, core, half),
                    rows_send.at[slot, half],
                    rows_recv.at[slot, half],
                    device,
                )
            )
    up_copies = [
        remote(ups_ref, ups_all_ref.at[x * 2 + core], ups_send.at[i], ups_recv.at[i], device)
        for i, device in enumerate(others[:3])
    ]

    sends = {}

    def gathered(kind):
        return packs_ref if kind == 0 else full_ref.at[kind - 1]

    def piece_at(flow, piece):
        kind, part, _, _ = FLOWS[flow]
        px, py = lax.rem(x + piece[0], 2), lax.rem(y + piece[1], 2)
        return gathered(kind).at[
            core, px, z + piece[2], py, pl.ds(part * part_rows, part_rows)
        ], (px * 2 + py) * DEPTH + z + piece[2]

    def handle(flow, piece):
        kind, part, order, _ = FLOWS[flow]
        landed, index = piece_at(flow, piece)
        source = landed
        if piece == OWN:
            source = shards[kind].at[pl.ds(part * part_rows, part_rows)]
        else:
            remote(landed, landed, send_sem.at[flow, 0], piece_recv.at[flow, index], place.sibling()).wait_recv()
        for axis, sign in forwards(order, piece):
            slot = {"x": 0, "y": 1, "z": 2 if sign > 0 else 3}[axis]
            copy = remote(
                source,
                landed,
                send_sem.at[flow, slot],
                piece_recv.at[flow, index],
                place.step(axis, sign),
            )
            if axis == "z":
                pl.when((z + sign >= 0) & (z + sign < DEPTH))(copy.start)
            else:
                copy.start()
                sends[flow, slot] = sends.get((flow, slot), 0) + 1
        remote(source, landed, sib_send.at[flow], sib_recv.at[flow], place.sibling()).start()

    def block_of(flow, pieces, plane):
        kind, part, _, _ = FLOWS[flow]
        nx = 2 if pieces % 2 == 0 else 1
        ny = 2 if pieces % 4 == 0 else 1
        return gathered(kind).at[
            plane,
            pl.ds(0, nx),
            pl.ds(0, pieces // (nx * ny)),
            pl.ds(0, ny),
            pl.ds(part * part_rows, part_rows),
        ]

    def finish_flow(flow):
        order = FLOWS[flow][2]
        everything = block_of(flow, 4 * DEPTH, 1 - core)
        remote(everything, everything, sib_send.at[flow], sib_recv.at[flow], place.sibling()).wait()

    def finish_sends(flow):
        order = FLOWS[flow][2]
        for axis, slot in (("x", 0), ("y", 1)):
            block = block_of(flow, 2 ** order.index(axis) * (DEPTH // 2 if "z" in order[: order.index(axis)] else 1), core)
            remote(block, block, send_sem.at[flow, slot], sib_recv.at[flow], place.sibling()).wait_send()
        each = 2 ** order.index("z")
        for at in range(DEPTH):
            for slot, sets in ((2, at + 1 if at < DEPTH - 1 else 0), (3, DEPTH - at if at > 0 else 0)):
                if sets:

                    @pl.when(z == at)
                    def _(slot=slot, sets=sets):
                        nx = 2 if each > 1 else 1
                        ny = 2 if each > 2 else 1
                        kind, part, _, _ = FLOWS[flow]
                        block = gathered(kind).at[
                            core,
                            pl.ds(0, nx),
                            pl.ds(0, sets),
                            pl.ds(0, ny),
                            pl.ds(part * part_rows, part_rows),
                        ]
                        remote(
                            block, block, send_sem.at[flow, slot], sib_recv.at[flow], place.sibling()
                        ).wait_send()

    for copy in row_copies + up_copies + own_copies:
        copy.start()

    def pass_rows(half):
        row_copies[2 * half].wait_recv()
        landed = rows_at(1 - x, core, half)
        copy = remote(landed, landed, rows_send.at[2, half], rows_recv.at[2, half], place.sibling())
        copy.start()
        return copy

    outs = []

    def write(source, target):
        copy = pltpu.make_async_copy(source, target, out_sem.at[len(outs)])
        copy.start()
        outs.append(copy)

    def assemble(t):
        if t == 0:
            for copy in up_copies + own_copies[:3]:
                copy.wait()
            for half in range(2):
                row_copies[2 * half + 1].wait_recv()
                passed_rows[half].wait_recv()
            for owner in range(4):
                write(rows_ref.at[owner], rows_hbm.at[pl.ds(owner * token_rows, token_rows)])
            finish_flow(0)
            finish_flow(1)
            for owner in range(4):
                ups_full[:, owner * slim : (owner + 1) * slim] = ups_all_ref[owner, :, :slim].astype(jnp.bfloat16)
        lanes = slice(t * slim, (t + 1) * slim)
        source = packs_ref.at[t % 2, t // 2]
        for kind, down_ref, first in ((0, down_q_ref, 0), (1, None, 0), (2, down_v_ref, 8), (3, None, 0)):
            part = source[:, :, :, kind * slim : (kind + 1) * slim].reshape(-1, slim)
            if down_ref is not None:
                up = ups_all_ref[t, first : first + 8, :slim].astype(jnp.bfloat16)
                product = dot_tn(down_ref[...], up)
                part = (part.astype(jnp.float32) + ADAPTER_SCALE * product).astype(jnp.bfloat16)
            weights_ref[kind, :, lanes] = part
        if t == 3:
            write(weights_ref, weights_hbm)

    def own_queries():
        q_ref[...] = dot_nn(rows_ref[x * 2 + core], weights_ref[0]).astype(jnp.bfloat16)
        write(q_ref, q_hbm)

    def keys_values(ref, hbm, kind, owner):
        ref[owner] = dot_nn(rows_ref[owner], weights_ref[kind]).astype(jnp.bfloat16)
        write(ref.at[owner], hbm.at[pl.ds(owner * token_rows, token_rows)])

    steps = [functools.partial(assemble, t) for t in range(4)] + [own_queries]
    for owner in range(4):
        steps.append(functools.partial(keys_values, k_ref, k_hbm, 1, owner))
        steps.append(functools.partial(keys_values, v_ref, v_hbm, 2, owner))

    passed_rows = []
    events = event_order(17.0)
    last_pack = max(i for i, (flow, _) in enumerate(events) if FLOWS[flow][0] == 0)
    between = max(1, (len(events) - last_pack) // (len(steps) + 1))
    arrivals = 0
    for at, (flow, piece) in enumerate(events):
        if piece[2] == 0:
            handle(flow, piece)
        else:
            pl.when((z + piece[2] >= 0) & (z + piece[2] < DEPTH))(
                functools.partial(handle, flow, piece)
            )
        if piece != OWN:
            arrivals += 1
            if arrivals in (8, 16):
                passed_rows.append(pass_rows(len(passed_rows)))
        if at >= last_pack and (at - last_pack) % between == between - 1 and steps:
            steps.pop(0)()
    for step in steps:
        step()

    for half in range(2):
        row_copies[2 * half].wait_send()
        row_copies[2 * half + 1].wait_send()
        passed_rows[half].wait_send()
    for copy in own_copies[3:] + outs:
        copy.wait()
    for flow in range(len(FLOWS)):
        if flow > 1:
            finish_flow(flow)
        finish_sends(flow)


def gather_all(w_q, w_k, w_v, w_out, w_in, w_down_t, tokens, up_q, up_v, down_q_t, down_v_t):
    shard_rows, width = w_in.shape
    token_rows = tokens.shape[0]
    bf16, f32 = jnp.bfloat16, jnp.float32
    slim = w_q.shape[1]
    padded = slim + -slim % 128
    flows = len(FLOWS)
    dma = pltpu.SemaphoreType.DMA
    grid = (2, 2, DEPTH, 2, shard_rows, width)
    return pl.pallas_call(
        gather_kernel,
        out_shape=(
            jax.ShapeDtypeStruct((2,) + grid, bf16),
            jax.ShapeDtypeStruct((4, width, width), bf16),
            jax.ShapeDtypeStruct((4 * token_rows, width), bf16),
            jax.ShapeDtypeStruct((token_rows, width), bf16),
            jax.ShapeDtypeStruct((4 * token_rows, width), bf16),
            jax.ShapeDtypeStruct((4 * token_rows, width), bf16),
            jax.ShapeDtypeStruct((16, width), bf16),
        ),
        in_specs=[VMEM_SPEC] * 4 + [HBM_SPEC] * 3 + [VMEM_SPEC] * 4,
        out_specs=(HBM_SPEC,) * 6 + (VMEM_SPEC,),
        scratch_shapes=[
            pltpu.VMEM((shard_rows, width), bf16),
            pltpu.VMEM(grid, bf16),
            pltpu.VMEM((4, token_rows, width), bf16),
            pltpu.VMEM((16, padded), f32),
            pltpu.VMEM((4, 16, padded), f32),
            pltpu.VMEM((4, width, width), bf16),
            pltpu.VMEM((token_rows, width), bf16),
            pltpu.VMEM((4, token_rows, width), bf16),
            pltpu.VMEM((4, token_rows, width), bf16),
            dma((flows, 4 * DEPTH)),
            dma((flows, 4)),
            dma((flows,)),
            dma((flows,)),
            dma((5,)),
            dma((3, 2)),
            dma((3, 2)),
            dma((3,)),
            dma((3,)),
            dma((14,)),
        ],
        compiler_params=pltpu.CompilerParams(
            collective_id=1, has_side_effects=True, vmem_limit_bytes=VMEM_LIMIT
        ),
        name="gather_all",
    )(w_q, w_k, w_v, w_out, w_in, w_down_t, tokens, up_q, up_v, down_q_t, down_v_t)


def project_kernel(
    order,
    full_hbm,
    rows_ref,
    ups_ref,
    downs_ref,
    weights_ref,
    q_ref,
    k_ref,
    v_ref,
    packs_ref,
    sems,
):
    token_rows = q_ref.shape[0]
    slim = packs_ref.shape[2] // 4
    tensor = lax.axis_index("tensor")
    copies = [
        pltpu.make_async_copy(full_hbm.at[0, i], packs_ref.at[i], sems.at[i])
        for i in range(len(order))
    ]
    for copy in copies:
        copy.start()
    for i, t in enumerate(order):
        copies[i].wait()
        lanes = slice(t * slim, (t + 1) * slim)
        for kind, first in ((0, 0), (1, None), (2, 8), (3, None)):
            part = packs_ref[i, :, kind * slim : (kind + 1) * slim]
            if first is not None:
                up = ups_ref[t, first : first + 8, :slim]
                product = dot_tn(downs_ref[first : first + 8, :], up)
                part = (part.astype(jnp.float32) + ADAPTER_SCALE * product).astype(jnp.bfloat16)
            weights_ref[kind, :, lanes] = part
    own = rows_ref[pl.ds(pl.multiple_of(tensor * token_rows, token_rows), token_rows), :]
    q_ref[...] = dot_nn(own, weights_ref[0]).astype(jnp.bfloat16)

    @pl.loop(0, rows_ref.shape[0] // token_rows)
    def _(at):
        window = pl.ds(pl.multiple_of(at * token_rows, token_rows), token_rows)
        block = rows_ref[window, :]
        k_ref[window, :] = dot_nn(block, weights_ref[1]).astype(jnp.bfloat16)
        v_ref[window, :] = dot_nn(block, weights_ref[2]).astype(jnp.bfloat16)


def project(order, full, rows_all, ups_all, downs, token_rows):
    total_rows, width = rows_all.shape
    bf16 = jnp.bfloat16
    return pl.pallas_call(
        functools.partial(project_kernel, order),
        out_shape=(
            jax.ShapeDtypeStruct((4, width, width), bf16),
            jax.ShapeDtypeStruct((token_rows, width), bf16),
            jax.ShapeDtypeStruct((total_rows, width), bf16),
            jax.ShapeDtypeStruct((total_rows, width), bf16),
        ),
        in_specs=[HBM_SPEC] + [VMEM_SPEC] * 3,
        out_specs=(VMEM_SPEC,) * 4,
        scratch_shapes=[
            pltpu.VMEM(full.shape[1:], bf16),
            pltpu.SemaphoreType.DMA((len(order),)),
        ],
        compiler_params=pltpu.CompilerParams(vmem_limit_bytes=VMEM_LIMIT),
        name="project",
    )(full, rows_all, ups_all, downs)


def ffn_kernel(
    tokens_ref,
    ctx_ref,
    cot_ref,
    gain_attn_ref,
    shift_attn_ref,
    gain_ffn_ref,
    shift_ffn_ref,
    weights_hbm,
    full_hbm,
    mixed_ref,
    grad_one_ref,
    grad_ctx_ref,
    out_buf,
    in_buf,
    down_buf,
    slope_buf,
    first_buf,
    sum_buf,
    normed_buf,
    inverse_buf,
    sems,
):
    parts, kinds = in_buf.shape[0], full_hbm.shape[0]
    blocks = tokens_ref.shape[0] // FFN_BLOCK
    gain_attn, shift_attn, gain_ffn, shift_ffn = (
        ref[...].reshape(1, -1) for ref in (gain_attn_ref, shift_attn_ref, gain_ffn_ref, shift_ffn_ref)
    )

    def out_copy():
        return pltpu.make_async_copy(weights_hbm.at[3], out_buf, sems.at[2 * parts])

    def in_copy(part):
        return pltpu.make_async_copy(full_hbm.at[kinds - 2, part], in_buf.at[part], sems.at[part])

    def down_copy(part):
        return pltpu.make_async_copy(
            full_hbm.at[kinds - 1, part], down_buf.at[part], sems.at[parts + part]
        )

    def block_rows(at):
        return pl.ds(pl.multiple_of(at * FFN_BLOCK, FFN_BLOCK), FFN_BLOCK)

    out_copy().start()
    for part in range(parts):
        in_copy(part).start()
        down_copy(part).start()
    out_copy().wait()

    @pl.loop(0, blocks)
    def _(at):
        rows = block_rows(at)
        residual = tokens_ref[rows, :].astype(jnp.float32) + dot_nt(ctx_ref[rows, :], out_buf[...])
        first, normed, inverse = norm_forward(residual, gain_attn, shift_attn)
        first_buf[rows, :] = first.astype(jnp.bfloat16)
        sum_buf[rows, :] = first.astype(jnp.bfloat16).astype(jnp.float32)
        normed_buf[rows, :] = normed
        inverse_buf[rows, :] = inverse

    @pl.loop(0, parts)
    def _(part):
        in_copy(part).wait()
        down_copy(part).wait()

        @pl.loop(0, blocks)
        def _(at):
            rows = block_rows(at)
            acted, slope = gelu_parts(dot_nn(first_buf[rows, :], in_buf[part]))
            slope_buf[part, rows, :] = slope
            sum_buf[rows, :] += dot_nt(acted.astype(jnp.bfloat16), down_buf[part])

    @pl.loop(0, blocks)
    def _(at):
        rows = block_rows(at)
        mixed, normed, inverse = norm_forward(sum_buf[rows, :], gain_ffn, shift_ffn)
        mixed_ref[rows, :] = mixed.astype(jnp.bfloat16)
        grad_two = norm_backward(cot_ref[rows, :].astype(jnp.float32), normed, inverse, gain_ffn)
        first_buf[rows, :] = grad_two.astype(jnp.bfloat16)
        sum_buf[rows, :] = grad_two

    @pl.loop(0, parts * blocks)
    def _(step):
        part, rows = step // blocks, block_rows(lax.rem(step, blocks))
        grad_hidden = dot_nn(first_buf[rows, :], down_buf[part]) * slope_buf[part, rows, :]
        sum_buf[rows, :] += dot_nt(grad_hidden.astype(jnp.bfloat16), in_buf[part])

    @pl.loop(0, blocks)
    def _(at):
        rows = block_rows(at)
        grad_one = norm_backward(
            sum_buf[rows, :], normed_buf[rows, :], inverse_buf[rows, :], gain_attn
        )
        grad_one_ref[rows, :] = grad_one
        grad_ctx_ref[rows, :] = dot_nn(grad_one.astype(jnp.bfloat16), out_buf[...]).astype(
            jnp.bfloat16
        )


def feed_forward(tokens, context, cotangent, norms, weights, full):
    rows, width = tokens.shape
    parts = full.shape[1]
    part_shape = full.shape[1:]
    return pl.pallas_call(
        ffn_kernel,
        out_shape=(
            jax.ShapeDtypeStruct((rows, width), jnp.bfloat16),
            jax.ShapeDtypeStruct((rows, width), jnp.float32),
            jax.ShapeDtypeStruct((rows, width), jnp.bfloat16),
        ),
        in_specs=[VMEM_SPEC] * 7 + [HBM_SPEC] * 2,
        out_specs=(VMEM_SPEC,) * 3,
        scratch_shapes=[
            pltpu.VMEM((width, width), jnp.bfloat16),
            pltpu.VMEM(part_shape, jnp.bfloat16),
            pltpu.VMEM(part_shape, jnp.bfloat16),
            pltpu.VMEM((parts, rows, part_shape[2]), jnp.float32),
            pltpu.VMEM((rows, width), jnp.bfloat16),
            pltpu.VMEM((rows, width), jnp.float32),
            pltpu.VMEM((rows, width), jnp.float32),
            pltpu.VMEM((rows, 1), jnp.float32),
            pltpu.SemaphoreType.DMA((1 + 2 * parts,)),
        ],
        compiler_params=pltpu.CompilerParams(vmem_limit_bytes=VMEM_LIMIT),
        name="feed_forward",
    )(tokens, context, cotangent, *norms, weights, full)


def adapter_parts(rows_ref, grad_ref, down_t, up, total_ref, down_at, up_at):
    block = 512
    first = jnp.zeros(down_t.shape, jnp.float32)
    second = jnp.zeros(down_t.shape, jnp.float32)
    for at in range(rows_ref.shape[0] // block):
        window = pl.ds(at * block, block)
        rows, grads = rows_ref[window, :], grad_ref[window, :]
        lifted = (ADAPTER_SCALE * dot_nt(rows, down_t)).astype(jnp.bfloat16)
        grad_lifted = (ADAPTER_SCALE * dot_nt(grads, up)).astype(jnp.bfloat16)
        second = second + dot_tn(lifted, grads)
        first = first + dot_tn(grad_lifted, rows)
    total_ref[down_at : down_at + 8, :] = first
    total_ref[up_at : up_at + 8, :] = second


def final_kernel(
    gq_hbm,
    gk_hbm,
    gv_hbm,
    weights_hbm,
    rows_hbm,
    grad_one_hbm,
    ups_full,
    down_q_ref,
    down_v_ref,
    grad_tokens_ref,
    aq_ref,
    av_ref,
    bq_ref,
    bv_ref,
    gq_ref,
    gk_ref,
    gv_ref,
    weights_ref,
    rows_ref,
    grad_one_ref,
    to_sib,
    from_sib,
    to_x,
    from_x,
    home_to,
    home_from,
    sums,
    sums_in,
    step_out,
    step_in,
    z_slots,
    final_in,
    load_sem,
    block_send,
    block_recv,
    sum_send,
    sum_recv,
):
    place = Place()
    x, y, z, core = place.x, place.y, place.z, place.core
    token_rows = gq_ref.shape[0]
    half_rows = token_rows // 2
    tensor = x * 2 + core

    def rows_of(block):
        return pl.ds(pl.multiple_of(block * token_rows, token_rows), token_rows)

    far_sib, far_same = (1 - x) * 2 + 1 - core, (1 - x) * 2 + core
    near_sib = x * 2 + 1 - core
    loads = {}

    def load(name, source, target):
        copy = pltpu.make_async_copy(source, target, load_sem.at[len(loads)])
        copy.start()
        loads[name] = copy

    for kind in (1, 2):
        load(("w", kind), weights_hbm.at[kind], weights_ref.at[kind])
    for block in range(4):
        owner = (far_sib, far_same, near_sib, tensor)[block]
        load(("k", block), gk_hbm.at[rows_of(owner)], gk_ref.at[rows_of(owner)])
        load(("v", block), gv_hbm.at[rows_of(owner)], gv_ref.at[rows_of(owner)])
    load("rows", rows_hbm, rows_ref)
    load("q", gq_hbm, gq_ref)
    load(("w", 0), weights_hbm.at[0], weights_ref.at[0])
    load("one", grad_one_hbm, grad_one_ref)

    barrier = pltpu.get_barrier_semaphore()
    others = [place.sibling(), place.step("x", 1), place.step("y", 1)]
    others += [place.device(z=lax.rem(z + i, DEPTH)) for i in range(1, DEPTH)]
    for target in others:
        pl.semaphore_signal(barrier, inc=1, device_id=target, device_id_type=MESH_ID)
    pl.semaphore_wait(barrier, len(others))

    def remote(source, target, send, recv, device):
        copy = pltpu.make_async_remote_copy(
            src_ref=source,
            dst_ref=target,
            send_sem=send,
            recv_sem=recv,
            device_id=device,
            device_id_type=MESH_ID,
        )
        copy.start()
        return copy

    slim = bq_ref.shape[1]

    def partial(owner, half):
        window = pl.ds(pl.multiple_of(owner * token_rows + half * half_rows, half_rows), half_rows)
        return dot_nt(gk_ref[window, :], weights_ref[1]) + dot_nt(gv_ref[window, :], weights_ref[2])

    def await_loads(*names):
        for name in names:
            loads[name].wait()

    await_loads(("w", 1), ("w", 2), ("k", 0), ("v", 0))
    sib_copies, x_copies, home_copies = [], [], []
    for half in range(2):
        to_sib[half] = partial(far_sib, half).astype(jnp.bfloat16)
        sib_copies.append(
            remote(
                to_sib.at[half],
                from_sib.at[half],
                block_send.at[0, half],
                block_recv.at[0, half],
                place.sibling(),
            )
        )
    await_loads(("k", 1), ("v", 1))
    for half in range(2):
        mine = partial(far_same, half)
        sib_copies[half].wait_recv()
        to_x[half] = (mine + from_sib[half].astype(jnp.float32)).astype(jnp.bfloat16)
        x_copies.append(
            remote(
                to_x.at[half],
                from_x.at[half],
                block_send.at[1, half],
                block_recv.at[1, half],
                place.step("x", 1),
            )
        )

    await_loads(("k", 2), ("v", 2), ("k", 3), ("v", 3), "rows", "q")
    own_rows = rows_ref.at[rows_of(tensor)]
    adapter_parts(own_rows, gq_ref, down_q_ref[...], ups_full[0:8, :], sums, 0, 16)
    adapter_parts(rows_ref, gv_ref, down_v_ref[...], ups_full[8:16, :], sums, 8, 24)
    kept = pl.ds(pl.multiple_of(core * 16, 16), 16)
    given = pl.ds(pl.multiple_of((1 - core) * 16, 16), 16)
    sum_copies = [
        remote(sums.at[given], sums_in, sum_send.at[0], sum_recv.at[0], place.sibling())
    ]
    for half in range(2):
        home_to[half] = partial(near_sib, half).astype(jnp.bfloat16)
        home_copies.append(
            remote(
                home_to.at[half],
                home_from.at[half],
                block_send.at[2, half],
                block_recv.at[2, half],
                place.sibling(),
            )
        )
    sum_copies[0].wait_recv()
    step_out[0] = sums[kept, :] + sums_in[...]
    sum_copies.append(
        remote(step_out.at[0], step_in.at[0], sum_send.at[1], sum_recv.at[1], place.step("y", 1))
    )
    await_loads(("w", 0), "one")
    for half in range(2):
        window = pl.ds(half * half_rows, half_rows)
        grad_one_ref[window, :] += partial(tensor, half) + dot_nt(gq_ref[window, :], weights_ref[0])
    sum_copies[1].wait_recv()
    z_slots[z] = step_out[0] + step_in[0]
    for i in range(1, DEPTH):
        there = lax.rem(z + i, DEPTH)
        sum_copies.append(
            remote(
                z_slots.at[z],
                z_slots.at[z],
                sum_send.at[1 + i],
                sum_recv.at[1 + i],
                place.device(z=there),
            )
        )
    for i in range(1, DEPTH):
        sum_copies[1 + i].wait_recv()
    column = z_slots[0]
    for i in range(1, DEPTH):
        column = column + z_slots[i]
    step_out[1] = column
    sum_copies.append(
        remote(
            step_out.at[1],
            step_in.at[1],
            sum_send.at[DEPTH + 1],
            sum_recv.at[DEPTH + 1],
            place.step("x", 1),
        )
    )
    sum_copies[-1].wait_recv()
    step_out[2] = step_out[1] + step_in[1]
    sum_copies.append(
        remote(
            step_out.at[2],
            final_in,
            sum_send.at[DEPTH + 2],
            sum_recv.at[DEPTH + 2],
            place.sibling(),
        )
    )

    for half in range(2):
        home_copies[half].wait_recv()
        x_copies[half].wait_recv()
        window = pl.ds(half * half_rows, half_rows)
        grad_tokens_ref[window, :] = (
            grad_one_ref[window, :]
            + home_from[half].astype(jnp.float32)
            + from_x[half].astype(jnp.float32)
        ).astype(jnp.bfloat16)
    sum_copies[-1].wait_recv()

    def give(first_half, second_half):
        aq_ref[...] = first_half[0:8, :]
        av_ref[...] = first_half[8:16, :]
        for t in range(4):

            @pl.when(tensor == t)
            def _(t=t):
                bq_ref[...] = second_half[0:8, t * slim : (t + 1) * slim]
                bv_ref[...] = second_half[8:16, t * slim : (t + 1) * slim]

    @pl.when(core == 0)
    def _():
        give(step_out.at[2], final_in)

    @pl.when(core == 1)
    def _():
        give(final_in, step_out.at[2])

    for copy in sib_copies + x_copies + home_copies + sum_copies:
        copy.wait_send()


def final_sums(
    grad_q, grad_k, grad_v, weights, rows_all, grad_one, ups_full, down_q_t, down_v_t, slim
):
    token_rows, width = grad_q.shape
    total_rows = grad_k.shape[0]
    bf16, f32 = jnp.bfloat16, jnp.float32
    half = (2, token_rows // 2, width)
    dma = pltpu.SemaphoreType.DMA
    return pl.pallas_call(
        final_kernel,
        out_shape=(
            jax.ShapeDtypeStruct((token_rows, width), bf16),
            jax.ShapeDtypeStruct((8, width), f32),
            jax.ShapeDtypeStruct((8, width), f32),
            jax.ShapeDtypeStruct((8, slim), f32),
            jax.ShapeDtypeStruct((8, slim), f32),
        ),
        in_specs=[HBM_SPEC] * 6 + [VMEM_SPEC] * 3,
        out_specs=(VMEM_SPEC,) * 5,
        scratch_shapes=[
            pltpu.VMEM((token_rows, width), bf16),
            pltpu.VMEM((total_rows, width), bf16),
            pltpu.VMEM((total_rows, width), bf16),
            pltpu.VMEM((3, width, width), bf16),
            pltpu.VMEM((total_rows, width), bf16),
            pltpu.VMEM((token_rows, width), f32),
        ]
        + [pltpu.VMEM(half, bf16)] * 6
        + [
            pltpu.VMEM((32, width), f32),
            pltpu.VMEM((16, width), f32),
            pltpu.VMEM((3, 16, width), f32),
            pltpu.VMEM((2, 16, width), f32),
            pltpu.VMEM((DEPTH, 16, width), f32),
            pltpu.VMEM((16, width), f32),
            dma((14,)),
            dma((3, 2)),
            dma((3, 2)),
            dma((DEPTH + 3,)),
            dma((DEPTH + 3,)),
        ],
        compiler_params=pltpu.CompilerParams(
            collective_id=2, has_side_effects=True, vmem_limit_bytes=VMEM_LIMIT
        ),
        name="final_sums",
    )(grad_q, grad_k, grad_v, weights, rows_all, grad_one, ups_full, down_q_t, down_v_t)


def local(
    fast,
    tokens,
    query_weight,
    w_key,
    value_weight,
    w_out,
    w_in,
    w_down,
    gain_attn,
    shift_attn,
    gain_ffn,
    shift_ffn,
    query_down_factor,
    query_up_factor,
    value_down_factor,
    value_up_factor,
    lengths,
    cotangent,
):
    slim = query_weight.shape[1]
    width = tokens.shape[1]
    token_rows = tokens.shape[0]
    down_q_t, down_v_t = query_down_factor.T, value_down_factor.T
    if fast:
        full, weights, rows_all, q_own, k_all, v_all, ups_full = gather_all(
            query_weight,
            w_key,
            value_weight,
            w_out,
            w_in,
            w_down.T,
            tokens,
            query_up_factor,
            value_up_factor,
            down_q_t,
            down_v_t,
        )
        full = full.reshape(2, 4, width, width)
    else:
        attn_pack = jnp.concatenate([query_weight, w_key, value_weight, w_out.T], axis=1)
        full = jnp.stack([attn_pack, w_in, w_down.T])
        full = lax.all_gather(full, "dp", axis=1, tiled=True)
        full = lax.all_gather(full, "tensor", axis=1)
        rows_all = lax.all_gather(tokens, "tensor").reshape(-1, width)
        ups = jnp.concatenate([query_up_factor, value_up_factor], axis=0)
        ups = jnp.pad(ups, ((0, 0), (0, -slim % 128)))
        ups_all = lax.all_gather(ups, "tensor")
        downs = jnp.concatenate([down_q_t, down_v_t], axis=0)
        order = tuple(range(full.shape[1]))
        weights, q_own, k_all, v_all = project(order, full, rows_all, ups_all, downs, token_rows)

    context, lse = attend_forward(lengths, q_own, k_all, v_all)
    norms = (gain_attn, shift_attn, gain_ffn, shift_ffn)
    mixed, grad_one, grad_context = feed_forward(
        tokens, context, cotangent, norms, weights, full
    )

    grad_q, grad_k, grad_v = attend_backward(
        lengths, q_own, k_all, v_all, context, lse, grad_context
    )
    if fast:
        grad_tokens, grad_aq, grad_av, grad_bq, grad_bv = final_sums(
            grad_q,
            grad_k,
            grad_v,
            weights,
            rows_all,
            grad_one,
            ups_full,
            down_q_t,
            down_v_t,
            slim,
        )
        return (mixed, grad_tokens, grad_aq.T, grad_bq, grad_av.T, grad_bv)

    query_up = ups_all[:, :8, :slim].transpose(1, 0, 2).reshape(8, width)
    value_up = ups_all[:, 8:, :slim].transpose(1, 0, 2).reshape(8, width)
    w_q, w_k, w_v = weights[0], weights[1], weights[2]
    u_query = dot_nn(tokens, query_down_factor).astype(jnp.bfloat16)
    u_value = dot_nn(rows_all, value_down_factor).astype(jnp.bfloat16)
    grad_uq = ADAPTER_SCALE * dot_nt(grad_q, query_up)
    grad_uv = ADAPTER_SCALE * dot_nt(grad_v, value_up)
    grad_bq = ADAPTER_SCALE * dot_tn(u_query, grad_q)
    grad_bv = ADAPTER_SCALE * dot_tn(u_value, grad_v)
    grad_aq = dot_tn(tokens, grad_uq.astype(jnp.bfloat16))
    grad_av = dot_tn(rows_all, grad_uv.astype(jnp.bfloat16))
    grad_rows = dot_nt(grad_k, w_k) + dot_nt(grad_v, w_v)
    own_rows = dot_nt(grad_q, w_q)
    shared = lax.psum_scatter(
        grad_rows.astype(jnp.bfloat16), "tensor", scatter_dimension=0, tiled=True
    )
    grad_tokens = (grad_one + own_rows + shared.astype(jnp.float32)).astype(jnp.bfloat16)
    grad_aq, grad_av, grad_bq, grad_bv = lax.psum(
        (grad_aq, grad_av, grad_bq, grad_bv), ("dp", "tensor")
    )
    at = lax.axis_index("tensor") * slim
    grad_bq = lax.dynamic_slice_in_dim(grad_bq, at, slim, 1)
    grad_bv = lax.dynamic_slice_in_dim(grad_bv, at, slim, 1)
    return (mixed, grad_tokens, grad_aq, grad_bq, grad_av, grad_bv)


def solution(mesh):
    fast = dict(mesh.shape) == {"dp": 2 * DEPTH, "tensor": 4}
    return jax.shard_map(
        functools.partial(local, fast),
        mesh=mesh,
        in_specs=(
            P(("dp", "tensor"), None),
            P("dp", "tensor"),
            P("dp", "tensor"),
            P("dp", "tensor"),
            P("tensor", "dp"),
            P("dp", "tensor"),
            P("tensor", "dp"),
            P(),
            P(),
            P(),
            P(),
            P(),
            P(None, "tensor"),
            P(),
            P(None, "tensor"),
            P("dp", None),
            P(("dp", "tensor"), None),
        ),
        out_specs=(
            P(("dp", "tensor"), None),
            P(("dp", "tensor"), None),
            P(),
            P(None, "tensor"),
            P(),
            P(None, "tensor"),
        ),
        check_vma=False,
    )
```

profile of v0, /device:TPU:0, one launch (start us, length us, event | category | flops | bytes accessed | tf_op | source)
XLA Modules:
  0.0 164.1 jit_solution(9878957903682021683)
XLA Ops:
  0.6 72.3 %gather_all.1 = (bf16[2,2,2,4,2,96,768]{6,5,4,3,2,1,0:T(8,128)(2,1)}, bf16[4,768,768]{2,1,0:T(8,128)(2,1)}, bf16[2048,768]{1,0:T(8,128)(2,1)}, bf16[512,768]{1,0...) custom-call(bf16[96,192]{1,0:T(8,128)(2,1)} %wq_ref.1, ...), custom_call_target="tpu_custom_call" | custom-call | tf_op jit(solution)/shard_map/gather_all/pallas_call | solution.py:647
  73.0 12.9 %attend_forward.1 = (bf16[512,768]{1,0:T(8,128)(2,1)}, f32[12,1,512]{2,1,0:T(1,128)}) custom-call(s32[1,32]{1,0:T(1,128)} %lengths_ref.3, bf16[512,768]{1,0:T(8,128)(2,1)} %get-tuple-element.26.q_ref, bf16[2048,768]{1,0:T(8,128)(2,1)} %get-tuple-element.27.k_ref, bf16[2048,768]{1,0:T(8,128)(2,1)} %get-tuple-element.28.v_ref), custom_call_target="tpu_custom_call" | custom-call | tf_op jit(solution)/shard_map/attend_forward/pallas_call | solution.py:249
  85.9 23.7 %feed_forward.1 = (bf16[512,768]{1,0:T(8,128)(2,1)}, f32[512,768]{1,0:T(8,128)}, bf16[512,768]{1,0:T(8,128)(2,1)}) custom-call(bf16[512,768]{1,0:T(8,128)(2,1)} %tokens_ref.3, bf16[512,768]{1,0:T(8,128)(2,1)} %get-tuple-element.29.ctx_ref, bf16[512,768]{1,0:T(8,128)(2,1)} %cot_ref.1, f32[768]{0:T(1024)} %gain_attn_ref.1, f32[768]{0:T(1024)} %shift_attn_ref.1, ...), custom_call_target="tpu_custom_call" | custom-call | tf_op jit(solution)/shard_map/feed_forward/pallas_call | solution.py:855
  109.5 19.0 %attend_backward.1 = (bf16[512,768]{1,0:T(8,128)(2,1)}, bf16[2048,768]{1,0:T(8,128)(2,1)}, bf16[2048,768]{1,0:T(8,128)(2,1)}) custom-call(s32[1,32]{1,0:T(1,128)} %lengths_ref.3, bf16[512,768]{1,0:T(8,128)(2,1)} %get-tuple-element.26.q_ref, bf16[2048,768]{1,0:T(8,128)(2,1)} %get-tuple-element.27.k_ref, bf16[2048,768]{1,0:T(8,128)(2,1)} %get-tuple-element.28.v_ref, ...), custom_call_target="tpu_custom_call" | custom-call | tf_op jit(solution)/shard_map/attend_backward/pallas_call | solution.py:265
  128.5 28.2 %final_sums.1 = (bf16[512,768]{1,0:T(8,128)(2,1)}, f32[8,768]{1,0:T(8,128)}, f32[8,768]{1,0:T(8,128)}, f32[8,192]{1,0:T(8,128)}, f32[8,192]{1,0:T(8,128)}) custom-call(bf16[512,768]{1,0:T(8,128)(2,1)} %get-tuple-element.35.gq_hbm, bf16[2048,768]{1,0:T(8,128)(2,1)} %get-tuple-element.36.gk_hbm, bf16[2048,768]{1,0:T(8,128)(2,1)} %get-tuple-element.37.gv_hbm, ...), custom_call_target="tpu_custom_call" | custom-call | tf_op jit(solution)/shard_map/final_sums/pallas_call | solution.py:1130
  156.7 2.1 %copy.28 = bf16[512,768]{1,0:T(8,128)(2,1)} copy(bf16[512,768]{1,0:T(8,128)(2,1)} %get-tuple-element.53) | data formatting | bytes 1572864
  158.8 1.3 copy.29
  160.1 1.3 copy.30
  161.4 1.3 copy.31
  162.8 1.3 copy.32
where the time goes:
time: 165 us; the launch traced here: 164 us
  Pallas kernels  156 us (95%)
  local copies, waits for them, and re-layouts  7.34 us (4%)
    pallas_call x1, Pallas kernels, gather_all(): pl.pallas_call(gather_kernel, out_shape=(jax.ShapeDtypeStruct((2,) + grid...  72.3 us
    pallas_call x1, Pallas kernels, final_sums(): pl.pallas_call(final_kernel, out_shape=(jax.ShapeDtypeStruct((token_rows,...  28.2 us
    pallas_call x1, Pallas kernels, feed_forward(): pl.pallas_call(ffn_kernel, out_shape=(jax.ShapeDtypeStruct((rows, width),...  23.7 us
    pallas_call x1, Pallas kernels, attend_backward(): pl.pallas_call(backward_kernel, out_shape=(jax.ShapeDtypeStruct((rows, wi...  19 us
    pallas_call x1, Pallas kernels, attend_forward(): pl.pallas_call(forward_kernel, out_shape=(jax.ShapeDtypeStruct((rows, wid...  12.9 us
    unnamed x5, local copies, waits for them, and re-layouts  7.34 us

commit v1 on v0

--- a/solution.py
+++ b/solution.py
@@ -12,7 +12,7 @@
 PAIR = 2 * HEAD_DIM
 Q_BLOCK = 256
 K_BLOCK = 512
-FFN_BLOCK = 256
+KV_BLOCK = 256
 FORWARD_GROUP = 3
 BACKWARD_GROUP = 3
 ADAPTER_SCALE = 2.0
@@ -20,7 +20,7 @@
 LOG2_SCALE = SCORE_SCALE * 1.4426950408889634
 NEG_FILL = -1e30
 LN_EPS = 1e-05
-VMEM_LIMIT = 56 * 1024 * 1024
+VMEM_LIMIT = 60 * 1024 * 1024
 
 
 def dot_nn(left, right):
@@ -118,15 +118,19 @@
     return start, (key_at >= jnp.maximum(begin, wanted)) & (key_at < finish)
 
 
+def query_span(lengths_ref, first_row, total_rows):
+    low, high = block_span(lengths_ref, first_row, Q_BLOCK, total_rows)
+    low = (low // 16) * 16
+    return low, (high - low + K_BLOCK - 1) // K_BLOCK
+
+
 def each_q_block(lengths_ref, rows, total_rows, group, heads_width, block_step):
     base = lax.axis_index("tensor") * rows
 
     @pl.loop(0, rows // Q_BLOCK)
     def _(q_at):
         first_row = base + q_at * Q_BLOCK
-        low, high = block_span(lengths_ref, first_row, Q_BLOCK, total_rows)
-        low = (low // 16) * 16
-        steps = (high - low + K_BLOCK - 1) // K_BLOCK
+        low, steps = query_span(lengths_ref, first_row, total_rows)
         begin, finish = row_bounds(lengths_ref, first_row, Q_BLOCK, total_rows)
         q_rows = pl.ds(pl.multiple_of(q_at * Q_BLOCK, Q_BLOCK), Q_BLOCK)
 
@@ -138,7 +142,7 @@
             block_step(q_rows, lanes, slots, low, steps, begin, finish)
 
 
-def forward_kernel(lengths_ref, q_ref, k_ref, v_ref, out_ref, lse_ref):
+def attend_forward(lengths_ref, q_ref, k_ref, v_ref, out_ref, lse_ref):
     total_rows = k_ref.shape[0]
 
     def block_step(q_rows, lanes, slots, low, steps, begin, finish):
@@ -174,23 +178,10 @@
     )
 
 
-def backward_kernel(
-    lengths_ref,
-    q_ref,
-    k_ref,
-    v_ref,
-    ctx_ref,
-    lse_ref,
-    grad_ref,
-    gq_ref,
-    gk_ref,
-    gv_ref,
-    gk_acc,
-    gv_acc,
+def attend_backward(
+    lengths_ref, q_ref, k_ref, v_ref, ctx_ref, lse_ref, grad_ref, gq_ref, gk_acc, gv_acc
 ):
     total_rows = k_ref.shape[0]
-    gk_acc[...] = jnp.zeros_like(gk_acc)
-    gv_acc[...] = jnp.zeros_like(gv_acc)
 
     def block_step(q_rows, lanes, slots, low, steps, begin, finish):
         ready = []
@@ -231,53 +222,10 @@
         lengths_ref, q_ref.shape[0], total_rows, BACKWARD_GROUP, q_ref.shape[1], block_step
     )
 
-    @pl.loop(0, total_rows // K_BLOCK)
-    def _(at):
-        window = pl.ds(pl.multiple_of(at * K_BLOCK, K_BLOCK), K_BLOCK)
-        gk_ref[window, :] = (gk_acc[window, :] * SCORE_SCALE).astype(jnp.bfloat16)
-        gv_ref[window, :] = gv_acc[window, :].astype(jnp.bfloat16)
-
 
 VMEM_SPEC = pl.BlockSpec(memory_space=pltpu.VMEM)
 HBM_SPEC = pl.BlockSpec(memory_space=pltpu.HBM)
 SMEM_SPEC = pl.BlockSpec(memory_space=pltpu.SMEM)
-
-
-def attend_forward(lengths, q_own, k_all, v_all):
-    rows, width = q_own.shape
-    heads = width // HEAD_DIM
-    return pl.pallas_call(
-        forward_kernel,
-        out_shape=(
-            jax.ShapeDtypeStruct((rows, width), jnp.bfloat16),
-            jax.ShapeDtypeStruct((rows // Q_BLOCK * heads // 2, 1, 2 * Q_BLOCK), jnp.float32),
-        ),
-        in_specs=[SMEM_SPEC] + [VMEM_SPEC] * 3,
-        out_specs=(VMEM_SPEC, VMEM_SPEC),
-        compiler_params=pltpu.CompilerParams(vmem_limit_bytes=VMEM_LIMIT),
-        name="attend_forward",
-    )(lengths, q_own, k_all, v_all)
-
-
-def attend_backward(lengths, q_own, k_all, v_all, context, lse, grad_context):
-    rows, width = q_own.shape
-    total_rows = k_all.shape[0]
-    return pl.pallas_call(
-        backward_kernel,
-        out_shape=(
-            jax.ShapeDtypeStruct((rows, width), jnp.bfloat16),
-            jax.ShapeDtypeStruct((total_rows, width), jnp.bfloat16),
-            jax.ShapeDtypeStruct((total_rows, width), jnp.bfloat16),
-        ),
-        in_specs=[SMEM_SPEC] + [VMEM_SPEC] * 6,
-        out_specs=(VMEM_SPEC,) * 3,
-        scratch_shapes=[
-            pltpu.VMEM((total_rows, width), jnp.float32),
-            pltpu.VMEM((total_rows, width), jnp.float32),
-        ],
-        compiler_params=pltpu.CompilerParams(vmem_limit_bytes=VMEM_LIMIT),
-        name="attend_backward",
-    )(lengths, q_own, k_all, v_all, context, lse, grad_context)
 
 
 MESH_ID = pl.DeviceIdType.MESH
@@ -750,19 +698,29 @@
     )(full, rows_all, ups_all, downs)
 
 
-def ffn_kernel(
-    tokens_ref,
-    ctx_ref,
-    cot_ref,
+def middle_kernel(
+    lengths_ref,
     gain_attn_ref,
     shift_attn_ref,
     gain_ffn_ref,
     shift_ffn_ref,
+    q_hbm,
+    k_hbm,
+    v_hbm,
+    tokens_hbm,
+    cot_hbm,
     weights_hbm,
     full_hbm,
-    mixed_ref,
-    grad_one_ref,
-    grad_ctx_ref,
+    mixed_hbm,
+    grad_one_hbm,
+    gq_hbm,
+    gk_hbm,
+    gv_hbm,
+    q_ref,
+    k_ref,
+    v_ref,
+    tokens_ref,
+    cot_ref,
     out_buf,
     in_buf,
     down_buf,
@@ -771,110 +729,215 @@
     sum_buf,
     normed_buf,
     inverse_buf,
-    sems,
+    ctx_ref,
+    lse_ref,
+    grad_ref,
+    gk_acc,
+    gv_acc,
+    gk_out,
+    gv_out,
+    load_sem,
+    part_sem,
+    kv_sem,
+    store_sem,
+    grad_sem,
 ):
+    rows, width = q_ref.shape
+    total_rows = k_ref.shape[0]
     parts, kinds = in_buf.shape[0], full_hbm.shape[0]
-    blocks = tokens_ref.shape[0] // FFN_BLOCK
+    kv_blocks = total_rows // KV_BLOCK
+    base = lax.axis_index("tensor") * rows
+
+    span_low, span_high = jnp.int32(total_rows), jnp.int32(0)
+    for at in range(rows // Q_BLOCK):
+        low, steps = query_span(lengths_ref, base + at * Q_BLOCK, total_rows)
+        span_low = jnp.minimum(span_low, jnp.minimum(low, total_rows - K_BLOCK))
+        span_high = jnp.maximum(span_high, jnp.minimum(low + steps * K_BLOCK, total_rows))
+
+    def kv_rows(block):
+        return pl.ds(pl.multiple_of(block * KV_BLOCK, KV_BLOCK), KV_BLOCK)
+
+    def touched(block):
+        return (block * KV_BLOCK < span_high) & ((block + 1) * KV_BLOCK > span_low)
+
+    def kv_copies(block):
+        window = kv_rows(block)
+        return (
+            pltpu.make_async_copy(k_hbm.at[window], k_ref.at[window], kv_sem.at[0, block]),
+            pltpu.make_async_copy(v_hbm.at[window], v_ref.at[window], kv_sem.at[1, block]),
+        )
+
+    def part_copies(part):
+        return (
+            pltpu.make_async_copy(
+                full_hbm.at[kinds - 2, part], in_buf.at[part], part_sem.at[0, part]
+            ),
+            pltpu.make_async_copy(
+                full_hbm.at[kinds - 1, part], down_buf.at[part], part_sem.at[1, part]
+            ),
+        )
+
+    q_copy = pltpu.make_async_copy(q_hbm, q_ref, load_sem.at[0])
+    tokens_copy = pltpu.make_async_copy(tokens_hbm, tokens_ref, load_sem.at[1])
+    out_copy = pltpu.make_async_copy(weights_hbm.at[3], out_buf, load_sem.at[2])
+    cot_copy = pltpu.make_async_copy(cot_hbm, cot_ref, load_sem.at[3])
+    q_copy.start()
+
+    @pl.loop(0, kv_blocks)
+    def _(block):
+        @pl.when(touched(block))
+        def _():
+            for copy in kv_copies(block):
+                copy.start()
+
+    tokens_copy.start()
+    out_copy.start()
+    cot_copy.start()
+    for part in range(parts):
+        for copy in part_copies(part):
+            copy.start()
+
+    gk_acc[...] = jnp.zeros_like(gk_acc)
+    gv_acc[...] = jnp.zeros_like(gv_acc)
+    q_copy.wait()
+
+    @pl.loop(0, kv_blocks)
+    def _(block):
+        @pl.when(touched(block))
+        def _():
+            for copy in kv_copies(block):
+                copy.wait()
+
+    attend_forward(lengths_ref, q_ref, k_ref, v_ref, ctx_ref, lse_ref)
+
     gain_attn, shift_attn, gain_ffn, shift_ffn = (
         ref[...].reshape(1, -1) for ref in (gain_attn_ref, shift_attn_ref, gain_ffn_ref, shift_ffn_ref)
     )
-
-    def out_copy():
-        return pltpu.make_async_copy(weights_hbm.at[3], out_buf, sems.at[2 * parts])
-
-    def in_copy(part):
-        return pltpu.make_async_copy(full_hbm.at[kinds - 2, part], in_buf.at[part], sems.at[part])
-
-    def down_copy(part):
-        return pltpu.make_async_copy(
-            full_hbm.at[kinds - 1, part], down_buf.at[part], sems.at[parts + part]
-        )
-
-    def block_rows(at):
-        return pl.ds(pl.multiple_of(at * FFN_BLOCK, FFN_BLOCK), FFN_BLOCK)
-
-    out_copy().start()
-    for part in range(parts):
-        in_copy(part).start()
-        down_copy(part).start()
-    out_copy().wait()
-
-    @pl.loop(0, blocks)
-    def _(at):
-        rows = block_rows(at)
-        residual = tokens_ref[rows, :].astype(jnp.float32) + dot_nt(ctx_ref[rows, :], out_buf[...])
-        first, normed, inverse = norm_forward(residual, gain_attn, shift_attn)
-        first_buf[rows, :] = first.astype(jnp.bfloat16)
-        sum_buf[rows, :] = first.astype(jnp.bfloat16).astype(jnp.float32)
-        normed_buf[rows, :] = normed
-        inverse_buf[rows, :] = inverse
+    tokens_copy.wait()
+    out_copy.wait()
+    residual = tokens_ref[...].astype(jnp.float32) + dot_nt(ctx_ref[...], out_buf[...])
+    first, normed, inverse = norm_forward(residual, gain_attn, shift_attn)
+    first_buf[...] = first.astype(jnp.bfloat16)
+    sum_buf[...] = first.astype(jnp.bfloat16).astype(jnp.float32)
+    normed_buf[...] = normed
+    inverse_buf[...] = inverse
 
     @pl.loop(0, parts)
     def _(part):
-        in_copy(part).wait()
-        down_copy(part).wait()
-
-        @pl.loop(0, blocks)
-        def _(at):
-            rows = block_rows(at)
-            acted, slope = gelu_parts(dot_nn(first_buf[rows, :], in_buf[part]))
-            slope_buf[part, rows, :] = slope
-            sum_buf[rows, :] += dot_nt(acted.astype(jnp.bfloat16), down_buf[part])
-
-    @pl.loop(0, blocks)
-    def _(at):
-        rows = block_rows(at)
-        mixed, normed, inverse = norm_forward(sum_buf[rows, :], gain_ffn, shift_ffn)
-        mixed_ref[rows, :] = mixed.astype(jnp.bfloat16)
-        grad_two = norm_backward(cot_ref[rows, :].astype(jnp.float32), normed, inverse, gain_ffn)
-        first_buf[rows, :] = grad_two.astype(jnp.bfloat16)
-        sum_buf[rows, :] = grad_two
-
-    @pl.loop(0, parts * blocks)
-    def _(step):
-        part, rows = step // blocks, block_rows(lax.rem(step, blocks))
-        grad_hidden = dot_nn(first_buf[rows, :], down_buf[part]) * slope_buf[part, rows, :]
-        sum_buf[rows, :] += dot_nt(grad_hidden.astype(jnp.bfloat16), in_buf[part])
-
-    @pl.loop(0, blocks)
-    def _(at):
-        rows = block_rows(at)
-        grad_one = norm_backward(
-            sum_buf[rows, :], normed_buf[rows, :], inverse_buf[rows, :], gain_attn
+        for copy in part_copies(part):
+            copy.wait()
+        acted, slope = gelu_parts(dot_nn(first_buf[...], in_buf[part]))
+        slope_buf[part] = slope
+        sum_buf[...] += dot_nt(acted.astype(jnp.bfloat16), down_buf[part])
+
+    cot_copy.wait()
+    mixed, normed, inverse = norm_forward(sum_buf[...], gain_ffn, shift_ffn)
+    tokens_ref[...] = mixed.astype(jnp.bfloat16)
+    mixed_copy = pltpu.make_async_copy(tokens_ref, mixed_hbm, store_sem.at[0])
+    mixed_copy.start()
+    grad_two = norm_backward(cot_ref[...].astype(jnp.float32), normed, inverse, gain_ffn)
+    first_buf[...] = grad_two.astype(jnp.bfloat16)
+    sum_buf[...] = grad_two
+
+    @pl.loop(0, parts)
+    def _(part):
+        grad_hidden = dot_nn(first_buf[...], down_buf[part]) * slope_buf[part]
+        sum_buf[...] += dot_nt(grad_hidden.astype(jnp.bfloat16), in_buf[part])
+
+    grad_one = norm_backward(sum_buf[...], normed_buf[...], inverse_buf[...], gain_attn)
+    normed_buf[...] = grad_one
+    grad_one_copy = pltpu.make_async_copy(normed_buf, grad_one_hbm, store_sem.at[1])
+    grad_one_copy.start()
+    grad_ref[...] = dot_nn(grad_one.astype(jnp.bfloat16), out_buf[...]).astype(jnp.bfloat16)
+
+    attend_backward(
+        lengths_ref, q_ref, k_ref, v_ref, ctx_ref, lse_ref, grad_ref, first_buf, gk_acc, gv_acc
+    )
+    gq_copy = pltpu.make_async_copy(first_buf, gq_hbm, store_sem.at[2])
+    gq_copy.start()
+
+    def grad_copies(block):
+        window = kv_rows(block)
+        return (
+            pltpu.make_async_copy(gk_out.at[window], gk_hbm.at[window], grad_sem.at[0, block]),
+            pltpu.make_async_copy(gv_out.at[window], gv_hbm.at[window], grad_sem.at[1, block]),
         )
-        grad_one_ref[rows, :] = grad_one
-        grad_ctx_ref[rows, :] = dot_nn(grad_one.astype(jnp.bfloat16), out_buf[...]).astype(
-            jnp.bfloat16
-        )
-
-
-def feed_forward(tokens, context, cotangent, norms, weights, full):
-    rows, width = tokens.shape
+
+    @pl.loop(0, kv_blocks)
+    def _(block):
+        window = kv_rows(block)
+
+        @pl.when(touched(block))
+        def _():
+            gk_out[window, :] = (gk_acc[window, :] * SCORE_SCALE).astype(jnp.bfloat16)
+            gv_out[window, :] = gv_acc[window, :].astype(jnp.bfloat16)
+
+        @pl.when(jnp.logical_not(touched(block)))
+        def _():
+            gk_out[window, :] = jnp.zeros((KV_BLOCK, width), jnp.bfloat16)
+            gv_out[window, :] = jnp.zeros((KV_BLOCK, width), jnp.bfloat16)
+
+        for copy in grad_copies(block):
+            copy.start()
+
+    for copy in (mixed_copy, grad_one_copy, gq_copy):
+        copy.wait()
+
+    @pl.loop(0, kv_blocks)
+    def _(block):
+        for copy in grad_copies(block):
+            copy.wait()
+
+
+def middle(lengths, norms, q_own, k_all, v_all, tokens, cotangent, weights, full):
+    rows, width = q_own.shape
+    total_rows = k_all.shape[0]
     parts = full.shape[1]
-    part_shape = full.shape[1:]
+    bf16, f32 = jnp.bfloat16, jnp.float32
+    slots = rows // Q_BLOCK * (width // PAIR)
+    kv_blocks = total_rows // KV_BLOCK
+    dma = pltpu.SemaphoreType.DMA
     return pl.pallas_call(
-        ffn_kernel,
+        middle_kernel,
         out_shape=(
-            jax.ShapeDtypeStruct((rows, width), jnp.bfloat16),
-            jax.ShapeDtypeStruct((rows, width), jnp.float32),
-            jax.ShapeDtypeStruct((rows, width), jnp.bfloat16),
+            jax.ShapeDtypeStruct((rows, width), bf16),
+            jax.ShapeDtypeStruct((rows, width), f32),
+            jax.ShapeDtypeStruct((rows, width), bf16),
+            jax.ShapeDtypeStruct((total_rows, width), bf16),
+            jax.ShapeDtypeStruct((total_rows, width), bf16),
         ),
-        in_specs=[VMEM_SPEC] * 7 + [HBM_SPEC] * 2,
-        out_specs=(VMEM_SPEC,) * 3,
+        in_specs=[SMEM_SPEC] + [VMEM_SPEC] * 4 + [HBM_SPEC] * 7,
+        out_specs=(HBM_SPEC,) * 5,
         scratch_shapes=[
-            pltpu.VMEM((width, width), jnp.bfloat16),
-            pltpu.VMEM(part_shape, jnp.bfloat16),
-            pltpu.VMEM(part_shape, jnp.bfloat16),
-            pltpu.VMEM((parts, rows, part_shape[2]), jnp.float32),
-            pltpu.VMEM((rows, width), jnp.bfloat16),
-            pltpu.VMEM((rows, width), jnp.float32),
-            pltpu.VMEM((rows, width), jnp.float32),
-            pltpu.VMEM((rows, 1), jnp.float32),
-            pltpu.SemaphoreType.DMA((1 + 2 * parts,)),
+            pltpu.VMEM((rows, width), bf16),
+            pltpu.VMEM((total_rows, width), bf16),
+            pltpu.VMEM((total_rows, width), bf16),
+            pltpu.VMEM((rows, width), bf16),
+            pltpu.VMEM((rows, width), bf16),
+            pltpu.VMEM((width, width), bf16),
+            pltpu.VMEM(full.shape[1:], bf16),
+            pltpu.VMEM(full.shape[1:], bf16),
+            pltpu.VMEM((parts, rows, full.shape[3]), f32),
+            pltpu.VMEM((rows, width), bf16),
+            pltpu.VMEM((rows, width), f32),
+            pltpu.VMEM((rows, width), f32),
+            pltpu.VMEM((rows, 1), f32),
+            pltpu.VMEM((rows, width), bf16),
+            pltpu.VMEM((slots, 1, 2 * Q_BLOCK), f32),
+            pltpu.VMEM((rows, width), bf16),
+            pltpu.VMEM((total_rows, width), f32),
+            pltpu.VMEM((total_rows, width), f32),
+            pltpu.VMEM((total_rows, width), bf16),
+            pltpu.VMEM((total_rows, width), bf16),
+            dma((4,)),
+            dma((2, parts)),
+            dma((2, kv_blocks)),
+            dma((3,)),
+            dma((2, kv_blocks)),
         ],
         compiler_params=pltpu.CompilerParams(vmem_limit_bytes=VMEM_LIMIT),
-        name="feed_forward",
-    )(tokens, context, cotangent, *norms, weights, full)
+        name="middle",
+    )(lengths, *norms, q_own, k_all, v_all, tokens, cotangent, weights, full)
 
 
 def adapter_parts(rows_ref, grad_ref, down_t, up, total_ref, down_at, up_at):
@@ -903,10 +966,7 @@
     down_q_ref,
     down_v_ref,
     grad_tokens_ref,
-    aq_ref,
-    av_ref,
-    bq_ref,
-    bv_ref,
+    sums_ref,
     gq_ref,
     gk_ref,
     gv_ref,
@@ -979,7 +1039,6 @@
         copy.start()
         return copy
 
-    slim = bq_ref.shape[1]
 
     def partial(owner, half):
         window = pl.ds(pl.multiple_of(owner * token_rows + half * half_rows, half_rows), half_rows)
@@ -1097,31 +1156,13 @@
         ).astype(jnp.bfloat16)
     sum_copies[-1].wait_recv()
 
-    def give(first_half, second_half):
-        aq_ref[...] = first_half[0:8, :]
-        av_ref[...] = first_half[8:16, :]
-        for t in range(4):
-
-            @pl.when(tensor == t)
-            def _(t=t):
-                bq_ref[...] = second_half[0:8, t * slim : (t + 1) * slim]
-                bv_ref[...] = second_half[8:16, t * slim : (t + 1) * slim]
-
-    @pl.when(core == 0)
-    def _():
-        give(step_out.at[2], final_in)
-
-    @pl.when(core == 1)
-    def _():
-        give(final_in, step_out.at[2])
-
+    for sums_half, half in ((step_out.at[2], core), (final_in, 1 - core)):
+        sums_ref[pl.ds(pl.multiple_of(half * 16, 16), 16), :] = sums_half[...]
     for copy in sib_copies + x_copies + home_copies + sum_copies:
         copy.wait_send()
 
 
-def final_sums(
-    grad_q, grad_k, grad_v, weights, rows_all, grad_one, ups_full, down_q_t, down_v_t, slim
-):
+def final_sums(grad_q, grad_k, grad_v, weights, rows_all, grad_one, ups_full, down_q_t, down_v_t):
     token_rows, width = grad_q.shape
     total_rows = grad_k.shape[0]
     bf16, f32 = jnp.bfloat16, jnp.float32
@@ -1131,13 +1172,10 @@
         final_kernel,
         out_shape=(
             jax.ShapeDtypeStruct((token_rows, width), bf16),
-            jax.ShapeDtypeStruct((8, width), f32),
-            jax.ShapeDtypeStruct((8, width), f32),
-            jax.ShapeDtypeStruct((8, slim), f32),
-            jax.ShapeDtypeStruct((8, slim), f32),
+            jax.ShapeDtypeStruct((32, width), f32),
         ),
         in_specs=[HBM_SPEC] * 6 + [VMEM_SPEC] * 3,
-        out_specs=(VMEM_SPEC,) * 5,
+        out_specs=(VMEM_SPEC,) * 2,
         scratch_shapes=[
             pltpu.VMEM((token_rows, width), bf16),
             pltpu.VMEM((total_rows, width), bf16),
@@ -1165,6 +1203,36 @@
         ),
         name="final_sums",
     )(grad_q, grad_k, grad_v, weights, rows_all, grad_one, ups_full, down_q_t, down_v_t)
+
+
+def hand_out_kernel(grad_ref, sums_ref, grad_out, aq_ref, av_ref, bq_ref, bv_ref):
+    grad_out[...] = grad_ref[...]
+    slim = bq_ref.shape[1]
+    aq_ref[...] = sums_ref[0:8, :]
+    av_ref[...] = sums_ref[8:16, :]
+    for t in range(sums_ref.shape[1] // slim):
+
+        @pl.when(lax.axis_index("tensor") == t)
+        def _(t=t):
+            bq_ref[...] = sums_ref[16:24, t * slim : (t + 1) * slim]
+            bv_ref[...] = sums_ref[24:32, t * slim : (t + 1) * slim]
+
+
+def hand_out(grad_tokens, sums, slim):
+    f32, width = jnp.float32, sums.shape[1]
+    return pl.pallas_call(
+        hand_out_kernel,
+        out_shape=(
+            jax.ShapeDtypeStruct(grad_tokens.shape, grad_tokens.dtype),
+            jax.ShapeDtypeStruct((8, width), f32),
+            jax.ShapeDtypeStruct((8, width), f32),
+            jax.ShapeDtypeStruct((8, slim), f32),
+            jax.ShapeDtypeStruct((8, slim), f32),
+        ),
+        in_specs=[VMEM_SPEC] * 2,
+        out_specs=(VMEM_SPEC,) * 5,
+        name="hand_out",
+    )(grad_tokens, sums)
 
 
 def local(
@@ -1219,28 +1287,15 @@
         order = tuple(range(full.shape[1]))
         weights, q_own, k_all, v_all = project(order, full, rows_all, ups_all, downs, token_rows)
 
-    context, lse = attend_forward(lengths, q_own, k_all, v_all)
     norms = (gain_attn, shift_attn, gain_ffn, shift_ffn)
-    mixed, grad_one, grad_context = feed_forward(
-        tokens, context, cotangent, norms, weights, full
-    )
-
-    grad_q, grad_k, grad_v = attend_backward(
-        lengths, q_own, k_all, v_all, context, lse, grad_context
+    mixed, grad_one, grad_q, grad_k, grad_v = middle(
+        lengths, norms, q_own, k_all, v_all, tokens, cotangent, weights, full
     )
     if fast:
-        grad_tokens, grad_aq, grad_av, grad_bq, grad_bv = final_sums(
-            grad_q,
-            grad_k,
-            grad_v,
-            weights,
-            rows_all,
-            grad_one,
-            ups_full,
-            down_q_t,
-            down_v_t,
-            slim,
+        grad_tokens, sums = final_sums(
+            grad_q, grad_k, grad_v, weights, rows_all, grad_one, ups_full, down_q_t, down_v_t
         )
+        grad_tokens, grad_aq, grad_av, grad_bq, grad_bv = hand_out(grad_tokens, sums, slim)
         return (mixed, grad_tokens, grad_aq.T, grad_bq, grad_av.T, grad_bv)
 
     query_up = ups_all[:, :8, :slim].transpose(1, 0, 2).reshape(8, width)

time: 165 us -> 146 us (0.88)
  Pallas kernels: 156 us -> 145 us
  local copies, waits for them, and re-layouts: 7.34 us -> 0 us
    pallas_call x3 -> x2, Pallas kernels: 55.6 us -> 44.6 us  [the longest x1 42.5 us: middle(): pl.pallas_call(middle_kernel, out_shape=(jax.ShapeDtypeStruct((rows, widt...]
    unnamed x5 -> x0, local copies, waits for them, and re-layouts: 7.34 us -> none
where the time goes in v1:
time: 146 us
  Pallas kernels  145 us (99%)
    pallas_call x1, Pallas kernels, gather_all(): pl.pallas_call(gather_kernel, out_shape=(jax.ShapeDtypeStruct((2,) + grid...  72.3 us
    pallas_call x1, Pallas kernels, middle(): pl.pallas_call(middle_kernel, out_shape=(jax.ShapeDtypeStruct((rows, widt...  42.5 us
    pallas_call x1, Pallas kernels, final_sums(): pl.pallas_call(final_kernel, out_shape=(jax.ShapeDtypeStruct((token_rows,...  28.4 us

profile of v1, /device:TPU:0, one launch (start us, length us, event | category | flops | bytes accessed | tf_op | source)
XLA Modules:
  0.0 146.0 jit_solution(7650544410555528909)
XLA Ops:
  0.6 72.3 %gather_all.1 = (bf16[2,2,2,4,2,96,768]{6,5,4,3,2,1,0:T(8,128)(2,1)}, bf16[4,768,768]{2,1,0:T(8,128)(2,1)}, bf16[2048,768]{1,0:T(8,128)(2,1)}, bf16[512,768]{1,0...) custom-call(bf16[96,192]{1,0:T(8,128)(2,1)} %wq_ref.1, ...), custom_call_target="tpu_custom_call" | custom-call | tf_op jit(solution)/shard_map/gather_all/pallas_call | solution.py:595
  73.0 42.5 %middle.1 = (bf16[512,768]{1,0:T(8,128)(2,1)}, f32[512,768]{1,0:T(8,128)}, bf16[512,768]{1,0:T(8,128)(2,1)}, bf16[2048,768]{1,0:T(8,128)(2,1)}, bf16[2048,768]{1,0:T(8,128)(2,1)}) custom-call(s32[1,32]{1,0:T(1,128)} %lengths_ref.1, f32[768]{0:T(1024)} %gain_attn_ref.1, f32[768]{0:T(1024)} %shift_attn_ref.1, f32[768]{0:T(1024)} %gain_ffn_ref.1, ...), custom_call_target="tpu_custom_call" | custom-call | tf_op jit(solution)/shard_map/middle/pallas_call | solution.py:900
  115.5 28.4 %final_sums.1 = (bf16[512,768]{1,0:T(8,128)(2,1)}, f32[32,768]{1,0:T(8,128)}) custom-call(bf16[512,768]{1,0:T(8,128)(2,1)} %get-tuple-element.31.gq_hbm, bf16[2048,768]{1,0:T(8,128)(2,1)} %get-tuple-element.32.gk_hbm, bf16[2048,768]{1,0:T(8,128)(2,1)} %get-tuple-element.33.gv_hbm, bf16[4,768,768]{2,1,0:T(8,128)(2,1)} %get-tuple-element.28.weights_hbm, ...), custom_call_target="tpu_custom_call" | custom-call | tf_op jit(solution)/shard_map/final_sums/pallas_call | solution.py:1171
  143.9 2.1 %hand_out.1 = (bf16[512,768]{1,0:T(8,128)(2,1)}, f32[8,768]{1,0:T(8,128)}, f32[8,768]{1,0:T(8,128)}, f32[8,192]{1,0:T(8,128)}, f32[8,192]{1,0:T(8,128)}) custom-call(bf16[512,768]{1,0:T(8,128)(2,1)} %get-tuple-element.37.grad_ref, f32[32,768]{1,0:T(8,128)} %get-tuple-element.38.sums_ref), custom_call_target="tpu_custom_call" | custom-call | tf_op jit(solution)/shard_map/hand_out/pallas_call | solution.py:1223

commit v2 on v1

--- a/solution.py
+++ b/solution.py
@@ -13,6 +13,7 @@
 Q_BLOCK = 256
 K_BLOCK = 512
 KV_BLOCK = 256
+FAR_CHUNKS = 4
 FORWARD_GROUP = 3
 BACKWARD_GROUP = 3
 ADAPTER_SCALE = 2.0
@@ -317,6 +318,7 @@
     up_v_ref,
     down_q_ref,
     down_v_ref,
+    lengths_ref,
     full_ref,
     weights_hbm,
     rows_hbm,
@@ -324,6 +326,7 @@
     k_hbm,
     v_hbm,
     ups_full,
+    fewest_ref,
     pack_ref,
     packs_ref,
     rows_ref,
@@ -333,6 +336,10 @@
     q_ref,
     k_ref,
     v_ref,
+    count_ref,
+    counts_ref,
+    count_send,
+    count_recv,
     piece_recv,
     send_sem,
     sib_send,
@@ -359,13 +366,9 @@
     )
     for target in others:
         pl.semaphore_signal(barrier, inc=1, device_id=target, device_id_type=MESH_ID)
-    for sign, there in ((1, z < DEPTH - 1), (-1, z > 0)):
-
-        @pl.when(there)
-        def _(sign=sign):
-            pl.semaphore_signal(
-                barrier, inc=1, device_id=place.step("z", sign), device_id_type=MESH_ID
-            )
+    column = [place.device(z=lax.rem(z + i, DEPTH)) for i in range(1, DEPTH)]
+    for target in column:
+        pl.semaphore_signal(barrier, inc=1, device_id=target, device_id_type=MESH_ID)
 
     slim = wq_ref.shape[1]
     for kind, ref in enumerate((wq_ref, wk_ref, wv_ref)):
@@ -374,9 +377,11 @@
     ups_ref[...] = jnp.zeros_like(ups_ref)
     ups_ref[0:8, :slim] = up_q_ref[...].astype(jnp.float32)
     ups_ref[8:16, :slim] = up_v_ref[...].astype(jnp.float32)
+    count_ref[...] = jnp.broadcast_to(
+        jnp.sum(lengths_ref[...].astype(jnp.float32), axis=1, keepdims=True), count_ref.shape
+    )
     shards = (pack_ref, w_in_ref, w_down_ref)
-    inner = ((z > 0) & (z < DEPTH - 1)).astype(jnp.int32)
-    pl.semaphore_wait(barrier, len(others) + 1 + inner)
+    pl.semaphore_wait(barrier, len(others) + len(column))
 
     def remote(source, target, send, recv, device):
         return pltpu.make_async_remote_copy(
@@ -421,19 +426,23 @@
     def gathered(kind):
         return packs_ref if kind == 0 else full_ref.at[kind - 1]
 
+    def half_of(kind, part):
+        return pl.ds(part * part_rows, part_rows)
+
     def piece_at(flow, piece):
         kind, part, _, _ = FLOWS[flow]
         px, py = lax.rem(x + piece[0], 2), lax.rem(y + piece[1], 2)
-        return gathered(kind).at[
-            core, px, z + piece[2], py, pl.ds(part * part_rows, part_rows)
-        ], (px * 2 + py) * DEPTH + z + piece[2]
+        return (
+            gathered(kind).at[core, px, z + piece[2], py, half_of(kind, part)],
+            (px * 2 + py) * DEPTH + z + piece[2],
+        )
 
     def handle(flow, piece):
         kind, part, order, _ = FLOWS[flow]
         landed, index = piece_at(flow, piece)
         source = landed
         if piece == OWN:
-            source = shards[kind].at[pl.ds(part * part_rows, part_rows)]
+            source = shards[kind].at[half_of(kind, part)]
         else:
             remote(landed, landed, send_sem.at[flow, 0], piece_recv.at[flow, index], place.sibling()).wait_recv()
         for axis, sign in forwards(order, piece):
@@ -461,7 +470,7 @@
             pl.ds(0, nx),
             pl.ds(0, pieces // (nx * ny)),
             pl.ds(0, ny),
-            pl.ds(part * part_rows, part_rows),
+            half_of(kind, part),
         ]
 
     def finish_flow(flow):
@@ -489,7 +498,7 @@
                             pl.ds(0, nx),
                             pl.ds(0, sets),
                             pl.ds(0, ny),
-                            pl.ds(part * part_rows, part_rows),
+                            half_of(kind, part),
                         ]
                         remote(
                             block, block, send_sem.at[flow, slot], sib_recv.at[flow], place.sibling()
@@ -497,6 +506,23 @@
 
     for copy in row_copies + up_copies + own_copies:
         copy.start()
+
+    count_copies = [
+        remote(
+            count_ref, counts_ref.at[DEPTH], count_send.at[0], count_recv.at[0], place.step("y", 1)
+        )
+    ]
+    count_copies[0].start()
+
+    def pass_count():
+        count_copies[0].wait_recv()
+        counts_ref[z] = jnp.minimum(count_ref[...], counts_ref[DEPTH])
+        for i, target in enumerate(column):
+            copy = remote(
+                counts_ref.at[z], counts_ref.at[z], count_send.at[1 + i], count_recv.at[1 + i], target
+            )
+            copy.start()
+            count_copies.append(copy)
 
     def pass_rows(half):
         row_copies[2 * half].wait_recv()
@@ -566,6 +592,8 @@
             arrivals += 1
             if arrivals in (8, 16):
                 passed_rows.append(pass_rows(len(passed_rows)))
+            if arrivals == 24:
+                pass_count()
         if at >= last_pack and (at - last_pack) % between == between - 1 and steps:
             steps.pop(0)()
     for step in steps:
@@ -581,9 +609,15 @@
         if flow > 1:
             finish_flow(flow)
         finish_sends(flow)
-
-
-def gather_all(w_q, w_k, w_v, w_out, w_in, w_down_t, tokens, up_q, up_v, down_q_t, down_v_t):
+    for copy in count_copies[1:]:
+        copy.wait()
+    count_copies[0].wait_send()
+    fewest_ref[0, 0] = jnp.min(counts_ref[0:DEPTH])
+
+
+def gather_all(
+    w_q, w_k, w_v, w_out, w_in, w_down_t, tokens, up_q, up_v, down_q_t, down_v_t, lengths
+):
     shard_rows, width = w_in.shape
     token_rows = tokens.shape[0]
     bf16, f32 = jnp.bfloat16, jnp.float32
@@ -602,9 +636,10 @@
             jax.ShapeDtypeStruct((4 * token_rows, width), bf16),
             jax.ShapeDtypeStruct((4 * token_rows, width), bf16),
             jax.ShapeDtypeStruct((16, width), bf16),
+            jax.ShapeDtypeStruct((1, 1), f32),
         ),
-        in_specs=[VMEM_SPEC] * 4 + [HBM_SPEC] * 3 + [VMEM_SPEC] * 4,
-        out_specs=(HBM_SPEC,) * 6 + (VMEM_SPEC,),
+        in_specs=[VMEM_SPEC] * 4 + [HBM_SPEC] * 3 + [VMEM_SPEC] * 5,
+        out_specs=(HBM_SPEC,) * 6 + (VMEM_SPEC, SMEM_SPEC),
         scratch_shapes=[
             pltpu.VMEM((shard_rows, width), bf16),
             pltpu.VMEM(grid, bf16),
@@ -615,6 +650,10 @@
             pltpu.VMEM((token_rows, width), bf16),
             pltpu.VMEM((4, token_rows, width), bf16),
             pltpu.VMEM((4, token_rows, width), bf16),
+            pltpu.VMEM((8, 128), f32),
+            pltpu.VMEM((DEPTH + 1, 8, 128), f32),
+            dma((DEPTH,)),
+            dma((DEPTH,)),
             dma((flows, 4 * DEPTH)),
             dma((flows, 4)),
             dma((flows,)),
@@ -630,7 +669,20 @@
             collective_id=1, has_side_effects=True, vmem_limit_bytes=VMEM_LIMIT
         ),
         name="gather_all",
-    )(w_q, w_k, w_v, w_out, w_in, w_down_t, tokens, up_q, up_v, down_q_t, down_v_t)
+    )(
+        w_q,
+        w_k,
+        w_v,
+        w_out,
+        w_in,
+        w_down_t,
+        tokens,
+        up_q,
+        up_v,
+        down_q_t,
+        down_v_t,
+        lengths,
+    )
 
 
 def project_kernel(
@@ -711,11 +763,17 @@
     cot_hbm,
     weights_hbm,
     full_hbm,
+    rows_hbm,
+    ups_ref,
+    down_q_ref,
+    down_v_ref,
     mixed_hbm,
     grad_one_hbm,
     gq_hbm,
     gk_hbm,
     gv_hbm,
+    far_hbm,
+    sums_hbm,
     q_ref,
     k_ref,
     v_ref,
@@ -736,11 +794,15 @@
     gv_acc,
     gk_out,
     gv_out,
+    far_out,
+    pair_buf,
+    sums_ref,
     load_sem,
     part_sem,
     kv_sem,
     store_sem,
     grad_sem,
+    far_sem,
 ):
     rows, width = q_ref.shape
     total_rows = k_ref.shape[0]
@@ -781,6 +843,7 @@
     tokens_copy = pltpu.make_async_copy(tokens_hbm, tokens_ref, load_sem.at[1])
     out_copy = pltpu.make_async_copy(weights_hbm.at[3], out_buf, load_sem.at[2])
     cot_copy = pltpu.make_async_copy(cot_hbm, cot_ref, load_sem.at[3])
+    pair_copy = pltpu.make_async_copy(weights_hbm.at[pl.ds(1, 2)], pair_buf, load_sem.at[4])
     q_copy.start()
 
     @pl.loop(0, kv_blocks)
@@ -796,6 +859,7 @@
     for part in range(parts):
         for copy in part_copies(part):
             copy.start()
+    pair_copy.start()
 
     gk_acc[...] = jnp.zeros_like(gk_acc)
     gv_acc[...] = jnp.zeros_like(gv_acc)
@@ -856,6 +920,16 @@
     gq_copy = pltpu.make_async_copy(first_buf, gq_hbm, store_sem.at[2])
     gq_copy.start()
 
+    def rows_copy(block):
+        window = kv_rows(block)
+        return pltpu.make_async_copy(rows_hbm.at[window], k_ref.at[window], kv_sem.at[0, block])
+
+    @pl.loop(0, kv_blocks)
+    def _(block):
+        @pl.when(touched(block))
+        def _():
+            rows_copy(block).start()
+
     def grad_copies(block):
         window = kv_rows(block)
         return (
@@ -880,6 +954,60 @@
         for copy in grad_copies(block):
             copy.start()
 
+    def far_copy(at):
+        window = kv_rows(at)
+        return pltpu.make_async_copy(far_out.at[window], far_hbm.at[window], far_sem.at[at])
+
+    pair_copy.wait()
+    tensor = lax.axis_index("tensor")
+    near = tensor // 2
+    per_owner = rows // KV_BLOCK
+
+    @pl.loop(0, kv_blocks // 2)
+    def _(at):
+        owner = (1 - near) * 2 + lax.rem(tensor + 1 + at // per_owner, 2)
+        block = owner * per_owner + lax.rem(at, per_owner)
+        source, target = kv_rows(block), kv_rows(at)
+
+        @pl.when(touched(block))
+        def _():
+            far_out[target, :] = (
+                dot_nt(gk_out[source, :], pair_buf[0]) + dot_nt(gv_out[source, :], pair_buf[1])
+            ).astype(jnp.bfloat16)
+
+        @pl.when(jnp.logical_not(touched(block)))
+        def _():
+            far_out[target, :] = jnp.zeros((KV_BLOCK, width), jnp.bfloat16)
+
+        far_copy(at).start()
+
+    def add_adapter(row_vals, grads, down, up, first_at, second_at):
+        lifted = (ADAPTER_SCALE * dot_nt(row_vals, down)).astype(jnp.bfloat16)
+        grad_lifted = (ADAPTER_SCALE * dot_nt(grads, up)).astype(jnp.bfloat16)
+        sums_ref[first_at : first_at + 8, :] += dot_tn(grad_lifted, row_vals)
+        sums_ref[second_at : second_at + 8, :] += dot_tn(lifted, grads)
+
+    sums_ref[...] = jnp.zeros_like(sums_ref)
+
+    @pl.loop(0, kv_blocks)
+    def _(block):
+        window = kv_rows(block)
+
+        @pl.when(touched(block))
+        def _():
+            rows_copy(block).wait()
+            add_adapter(k_ref[window, :], gv_out[window, :], down_v_ref[...], ups_ref[8:16, :], 8, 24)
+
+    own = pl.ds(pl.multiple_of(base, rows), rows)
+    add_adapter(k_ref[own, :], first_buf[...], down_q_ref[...], ups_ref[0:8, :], 0, 16)
+    sums_copy = pltpu.make_async_copy(sums_ref, sums_hbm, store_sem.at[3])
+    sums_copy.start()
+    sums_copy.wait()
+
+    @pl.loop(0, kv_blocks // 2)
+    def _(at):
+        far_copy(at).wait()
+
     for copy in (mixed_copy, grad_one_copy, gq_copy):
         copy.wait()
 
@@ -889,7 +1017,9 @@
             copy.wait()
 
 
-def middle(lengths, norms, q_own, k_all, v_all, tokens, cotangent, weights, full):
+def middle(
+    lengths, norms, q_own, k_all, v_all, tokens, cotangent, weights, full, rows_all, ups, downs
+):
     rows, width = q_own.shape
     total_rows = k_all.shape[0]
     parts = full.shape[1]
@@ -905,9 +1035,11 @@
             jax.ShapeDtypeStruct((rows, width), bf16),
             jax.ShapeDtypeStruct((total_rows, width), bf16),
             jax.ShapeDtypeStruct((total_rows, width), bf16),
+            jax.ShapeDtypeStruct((total_rows // 2, width), bf16),
+            jax.ShapeDtypeStruct((32, width), f32),
         ),
-        in_specs=[SMEM_SPEC] + [VMEM_SPEC] * 4 + [HBM_SPEC] * 7,
-        out_specs=(HBM_SPEC,) * 5,
+        in_specs=[SMEM_SPEC] + [VMEM_SPEC] * 4 + [HBM_SPEC] * 8 + [VMEM_SPEC] * 3,
+        out_specs=(HBM_SPEC,) * 7,
         scratch_shapes=[
             pltpu.VMEM((rows, width), bf16),
             pltpu.VMEM((total_rows, width), bf16),
@@ -929,63 +1061,65 @@
             pltpu.VMEM((total_rows, width), f32),
             pltpu.VMEM((total_rows, width), bf16),
             pltpu.VMEM((total_rows, width), bf16),
-            dma((4,)),
+            pltpu.VMEM((total_rows // 2, width), bf16),
+            pltpu.VMEM((2, width, width), bf16),
+            pltpu.VMEM((32, width), f32),
+            dma((5,)),
             dma((2, parts)),
             dma((2, kv_blocks)),
-            dma((3,)),
+            dma((4,)),
             dma((2, kv_blocks)),
+            dma((kv_blocks // 2,)),
         ],
         compiler_params=pltpu.CompilerParams(vmem_limit_bytes=VMEM_LIMIT),
         name="middle",
-    )(lengths, *norms, q_own, k_all, v_all, tokens, cotangent, weights, full)
-
-
-def adapter_parts(rows_ref, grad_ref, down_t, up, total_ref, down_at, up_at):
-    block = 512
-    first = jnp.zeros(down_t.shape, jnp.float32)
-    second = jnp.zeros(down_t.shape, jnp.float32)
-    for at in range(rows_ref.shape[0] // block):
-        window = pl.ds(at * block, block)
-        rows, grads = rows_ref[window, :], grad_ref[window, :]
-        lifted = (ADAPTER_SCALE * dot_nt(rows, down_t)).astype(jnp.bfloat16)
-        grad_lifted = (ADAPTER_SCALE * dot_nt(grads, up)).astype(jnp.bfloat16)
-        second = second + dot_tn(lifted, grads)
-        first = first + dot_tn(grad_lifted, rows)
-    total_ref[down_at : down_at + 8, :] = first
-    total_ref[up_at : up_at + 8, :] = second
+    )(
+        lengths,
+        *norms,
+        q_own,
+        k_all,
+        v_all,
+        tokens,
+        cotangent,
+        weights,
+        full,
+        rows_all,
+        ups,
+        *downs,
+    )
 
 
 def final_kernel(
+    reach,
     gq_hbm,
     gk_hbm,
     gv_hbm,
+    far_hbm,
     weights_hbm,
-    rows_hbm,
     grad_one_hbm,
-    ups_full,
-    down_q_ref,
-    down_v_ref,
+    part_sums,
     grad_tokens_ref,
     sums_ref,
     gq_ref,
     gk_ref,
     gv_ref,
+    far_ref,
     weights_ref,
-    rows_ref,
     grad_one_ref,
-    to_sib,
     from_sib,
     to_x,
     from_x,
     home_to,
     home_from,
-    sums,
     sums_in,
+    total,
+    total_in,
     step_out,
     step_in,
     z_slots,
-    final_in,
     load_sem,
+    far_send,
+    far_recv,
     block_send,
     block_recv,
     sum_send,
@@ -995,13 +1129,8 @@
     x, y, z, core = place.x, place.y, place.z, place.core
     token_rows = gq_ref.shape[0]
     half_rows = token_rows // 2
-    tensor = x * 2 + core
-
-    def rows_of(block):
-        return pl.ds(pl.multiple_of(block * token_rows, token_rows), token_rows)
-
-    far_sib, far_same = (1 - x) * 2 + 1 - core, (1 - x) * 2 + core
-    near_sib = x * 2 + 1 - core
+    chunk_rows = token_rows // FAR_CHUNKS
+    bf16, f32 = jnp.bfloat16, jnp.float32
     loads = {}
 
     def load(name, source, target):
@@ -1009,26 +1138,34 @@
         copy.start()
         loads[name] = copy
 
-    for kind in (1, 2):
-        load(("w", kind), weights_hbm.at[kind], weights_ref.at[kind])
-    for block in range(4):
-        owner = (far_sib, far_same, near_sib, tensor)[block]
-        load(("k", block), gk_hbm.at[rows_of(owner)], gk_ref.at[rows_of(owner)])
-        load(("v", block), gv_hbm.at[rows_of(owner)], gv_ref.at[rows_of(owner)])
-    load("rows", rows_hbm, rows_ref)
+    if reach:
+        load("far", far_hbm.at[pl.ds(token_rows, token_rows)], far_ref)
+    near_rows = pl.ds(pl.multiple_of(x * 2 * token_rows, token_rows), 2 * token_rows)
+    load("k", gk_hbm.at[near_rows], gk_ref)
+    load("v", gv_hbm.at[near_rows], gv_ref)
+    load("w", weights_hbm.at[pl.ds(0, 3)], weights_ref)
     load("q", gq_hbm, gq_ref)
-    load(("w", 0), weights_hbm.at[0], weights_ref.at[0])
     load("one", grad_one_hbm, grad_one_ref)
 
+    across = place.device(x=1 - x, core=1 - core)
+    middle_device = x != core
     barrier = pltpu.get_barrier_semaphore()
     others = [place.sibling(), place.step("x", 1), place.step("y", 1)]
     others += [place.device(z=lax.rem(z + i, DEPTH)) for i in range(1, DEPTH)]
     for target in others:
         pl.semaphore_signal(barrier, inc=1, device_id=target, device_id_type=MESH_ID)
-    pl.semaphore_wait(barrier, len(others))
+    greeted = len(others)
+    if not reach:
+
+        @pl.when(middle_device)
+        def _():
+            pl.semaphore_signal(barrier, inc=1, device_id=across, device_id_type=MESH_ID)
+
+        greeted = greeted + middle_device.astype(jnp.int32)
+    pl.semaphore_wait(barrier, greeted)
 
     def remote(source, target, send, recv, device):
-        copy = pltpu.make_async_remote_copy(
+        return pltpu.make_async_remote_copy(
             src_ref=source,
             dst_ref=target,
             send_sem=send,
@@ -1036,96 +1173,114 @@
             device_id=device,
             device_id_type=MESH_ID,
         )
+
+    def started(*operands):
+        copy = remote(*operands)
         copy.start()
         return copy
 
-
-    def partial(owner, half):
-        window = pl.ds(pl.multiple_of(owner * token_rows + half * half_rows, half_rows), half_rows)
-        return dot_nt(gk_ref[window, :], weights_ref[1]) + dot_nt(gv_ref[window, :], weights_ref[2])
-
-    def await_loads(*names):
-        for name in names:
-            loads[name].wait()
-
-    await_loads(("w", 1), ("w", 2), ("k", 0), ("v", 0))
-    sib_copies, x_copies, home_copies = [], [], []
-    for half in range(2):
-        to_sib[half] = partial(far_sib, half).astype(jnp.bfloat16)
-        sib_copies.append(
-            remote(
-                to_sib.at[half],
-                from_sib.at[half],
-                block_send.at[0, half],
-                block_recv.at[0, half],
-                place.sibling(),
-            )
-        )
-    await_loads(("k", 1), ("v", 1))
-    for half in range(2):
-        mine = partial(far_same, half)
-        sib_copies[half].wait_recv()
-        to_x[half] = (mine + from_sib[half].astype(jnp.float32)).astype(jnp.bfloat16)
-        x_copies.append(
-            remote(
-                to_x.at[half],
-                from_x.at[half],
-                block_send.at[1, half],
-                block_recv.at[1, half],
-                place.step("x", 1),
-            )
-        )
-
-    await_loads(("k", 2), ("v", 2), ("k", 3), ("v", 3), "rows", "q")
-    own_rows = rows_ref.at[rows_of(tensor)]
-    adapter_parts(own_rows, gq_ref, down_q_ref[...], ups_full[0:8, :], sums, 0, 16)
-    adapter_parts(rows_ref, gv_ref, down_v_ref[...], ups_full[8:16, :], sums, 8, 24)
+    chunks = [pl.ds(at * chunk_rows, chunk_rows) for at in range(FAR_CHUNKS)]
     kept = pl.ds(pl.multiple_of(core * 16, 16), 16)
     given = pl.ds(pl.multiple_of((1 - core) * 16, 16), 16)
     sum_copies = [
-        remote(sums.at[given], sums_in, sum_send.at[0], sum_recv.at[0], place.sibling())
+        started(part_sums.at[given], sums_in, sum_send.at[0], sum_recv.at[0], place.sibling())
     ]
-    for half in range(2):
-        home_to[half] = partial(near_sib, half).astype(jnp.bfloat16)
-        home_copies.append(
-            remote(
-                home_to.at[half],
-                home_from.at[half],
-                block_send.at[2, half],
-                block_recv.at[2, half],
-                place.sibling(),
+    sib_copies, x_copies = [], []
+    if reach:
+        for at, chunk in enumerate(chunks):
+            sib_copies.append(
+                started(
+                    far_hbm.at[chunk],
+                    from_sib.at[chunk],
+                    far_send.at[0, at],
+                    far_recv.at[0, at],
+                    place.sibling(),
+                )
             )
-        )
+    else:
+        for at, chunk in enumerate(chunks):
+            x_copies.append(
+                remote(
+                    far_hbm.at[chunk],
+                    from_x.at[chunk],
+                    far_send.at[1, at],
+                    far_recv.at[1, at],
+                    across,
+                )
+            )
+
+        @pl.when(middle_device)
+        def _():
+            for copy in x_copies:
+                copy.start()
+
+        @pl.when(jnp.logical_not(middle_device))
+        def _():
+            from_x[...] = jnp.zeros_like(from_x)
+
     sum_copies[0].wait_recv()
-    step_out[0] = sums[kept, :] + sums_in[...]
+    step_out[0] = (part_sums[kept, :] + sums_in[...]).astype(bf16)
     sum_copies.append(
-        remote(step_out.at[0], step_in.at[0], sum_send.at[1], sum_recv.at[1], place.step("y", 1))
-    )
-    await_loads(("w", 0), "one")
-    for half in range(2):
-        window = pl.ds(half * half_rows, half_rows)
-        grad_one_ref[window, :] += partial(tensor, half) + dot_nt(gq_ref[window, :], weights_ref[0])
+        started(step_out.at[0], step_in.at[0], sum_send.at[1], sum_recv.at[1], place.step("y", 1))
+    )
+    if reach:
+        loads["far"].wait()
+        for at, chunk in enumerate(chunks):
+            sib_copies[at].wait_recv()
+            to_x[chunk, :] = (far_ref[chunk, :].astype(f32) + from_sib[chunk, :].astype(f32)).astype(
+                bf16
+            )
+            x_copies.append(
+                started(
+                    to_x.at[chunk],
+                    from_x.at[chunk],
+                    far_send.at[1, at],
+                    far_recv.at[1, at],
+                    place.step("x", 1),
+                )
+            )
+
     sum_copies[1].wait_recv()
-    z_slots[z] = step_out[0] + step_in[0]
+    z_slots[z] = (step_out[0].astype(f32) + step_in[0].astype(f32)).astype(bf16)
     for i in range(1, DEPTH):
-        there = lax.rem(z + i, DEPTH)
         sum_copies.append(
-            remote(
+            started(
                 z_slots.at[z],
                 z_slots.at[z],
                 sum_send.at[1 + i],
                 sum_recv.at[1 + i],
-                place.device(z=there),
+                place.device(z=lax.rem(z + i, DEPTH)),
             )
         )
+
+    def partial(owner, half):
+        window = pl.ds(pl.multiple_of(owner * token_rows + half * half_rows, half_rows), half_rows)
+        return dot_nt(gk_ref[window, :], weights_ref[1]) + dot_nt(gv_ref[window, :], weights_ref[2])
+
+    for name in ("k", "v", "w"):
+        loads[name].wait()
+    home_copies = []
+    for half in range(2):
+        window = pl.ds(half * half_rows, half_rows)
+        home_to[window, :] = partial(1 - core, half).astype(bf16)
+        home_copies.append(
+            started(
+                home_to.at[window],
+                home_from.at[window],
+                block_send.at[half],
+                block_recv.at[half],
+                place.sibling(),
+            )
+        )
+
     for i in range(1, DEPTH):
         sum_copies[1 + i].wait_recv()
-    column = z_slots[0]
+    column = z_slots[0].astype(f32)
     for i in range(1, DEPTH):
-        column = column + z_slots[i]
-    step_out[1] = column
+        column = column + z_slots[i].astype(f32)
+    step_out[1] = column.astype(bf16)
     sum_copies.append(
-        remote(
+        started(
             step_out.at[1],
             step_in.at[1],
             sum_send.at[DEPTH + 1],
@@ -1133,76 +1288,84 @@
             place.step("x", 1),
         )
     )
+    for name in ("q", "one"):
+        loads[name].wait()
+    for half in range(2):
+        window = pl.ds(half * half_rows, half_rows)
+        grad_one_ref[window, :] += partial(core, half) + dot_nt(gq_ref[window, :], weights_ref[0])
     sum_copies[-1].wait_recv()
-    step_out[2] = step_out[1] + step_in[1]
+    total[...] = step_out[1].astype(f32) + step_in[1].astype(f32)
     sum_copies.append(
-        remote(
-            step_out.at[2],
-            final_in,
-            sum_send.at[DEPTH + 2],
-            sum_recv.at[DEPTH + 2],
-            place.sibling(),
-        )
-    )
-
-    for half in range(2):
-        home_copies[half].wait_recv()
-        x_copies[half].wait_recv()
-        window = pl.ds(half * half_rows, half_rows)
-        grad_tokens_ref[window, :] = (
-            grad_one_ref[window, :]
-            + home_from[half].astype(jnp.float32)
-            + from_x[half].astype(jnp.float32)
-        ).astype(jnp.bfloat16)
+        started(total, total_in, sum_send.at[DEPTH + 2], sum_recv.at[DEPTH + 2], place.sibling())
+    )
+
+    for copy in home_copies:
+        copy.wait_recv()
+    for at, chunk in enumerate(chunks):
+        if reach:
+            x_copies[at].wait_recv()
+        else:
+            pl.when(middle_device)(x_copies[at].wait_recv)
+        grad_tokens_ref[chunk, :] = (
+            grad_one_ref[chunk, :] + home_from[chunk, :].astype(f32) + from_x[chunk, :].astype(f32)
+        ).astype(bf16)
     sum_copies[-1].wait_recv()
-
-    for sums_half, half in ((step_out.at[2], core), (final_in, 1 - core)):
-        sums_ref[pl.ds(pl.multiple_of(half * 16, 16), 16), :] = sums_half[...]
-    for copy in sib_copies + x_copies + home_copies + sum_copies:
+    sums_ref[kept, :] = total[...]
+    sums_ref[given, :] = total_in[...]
+
+    for copy in sib_copies + home_copies + sum_copies:
         copy.wait_send()
-
-
-def final_sums(grad_q, grad_k, grad_v, weights, rows_all, grad_one, ups_full, down_q_t, down_v_t):
+    for copy in x_copies:
+        if reach:
+            copy.wait_send()
+        else:
+            pl.when(middle_device)(copy.wait_send)
+
+
+def final_sums(reach, grad_q, grad_k, grad_v, far_rows, weights, grad_one, sums):
     token_rows, width = grad_q.shape
-    total_rows = grad_k.shape[0]
     bf16, f32 = jnp.bfloat16, jnp.float32
-    half = (2, token_rows // 2, width)
     dma = pltpu.SemaphoreType.DMA
+    block = pltpu.VMEM((token_rows, width), bf16)
     return pl.pallas_call(
-        final_kernel,
+        functools.partial(final_kernel, reach),
         out_shape=(
             jax.ShapeDtypeStruct((token_rows, width), bf16),
             jax.ShapeDtypeStruct((32, width), f32),
         ),
-        in_specs=[HBM_SPEC] * 6 + [VMEM_SPEC] * 3,
+        in_specs=[HBM_SPEC] * 6 + [VMEM_SPEC],
         out_specs=(VMEM_SPEC,) * 2,
         scratch_shapes=[
-            pltpu.VMEM((token_rows, width), bf16),
-            pltpu.VMEM((total_rows, width), bf16),
-            pltpu.VMEM((total_rows, width), bf16),
+            block,
+            pltpu.VMEM((2 * token_rows, width), bf16),
+            pltpu.VMEM((2 * token_rows, width), bf16),
+            block,
             pltpu.VMEM((3, width, width), bf16),
-            pltpu.VMEM((total_rows, width), bf16),
             pltpu.VMEM((token_rows, width), f32),
-        ]
-        + [pltpu.VMEM(half, bf16)] * 6
-        + [
-            pltpu.VMEM((32, width), f32),
+            block,
+            block,
+            block,
+            block,
+            block,
             pltpu.VMEM((16, width), f32),
-            pltpu.VMEM((3, 16, width), f32),
-            pltpu.VMEM((2, 16, width), f32),
-            pltpu.VMEM((DEPTH, 16, width), f32),
             pltpu.VMEM((16, width), f32),
-            dma((14,)),
-            dma((3, 2)),
-            dma((3, 2)),
+            pltpu.VMEM((16, width), f32),
+            pltpu.VMEM((2, 16, width), bf16),
+            pltpu.VMEM((2, 16, width), bf16),
+            pltpu.VMEM((DEPTH, 16, width), bf16),
+            dma((6,)),
+            dma((2, FAR_CHUNKS)),
+            dma((2, FAR_CHUNKS)),
+            dma((2,)),
+            dma((2,)),
             dma((DEPTH + 3,)),
             dma((DEPTH + 3,)),
         ],
         compiler_params=pltpu.CompilerParams(
-            collective_id=2, has_side_effects=True, vmem_limit_bytes=VMEM_LIMIT
+            collective_id=2 if reach else 3, has_side_effects=True, vmem_limit_bytes=VMEM_LIMIT
         ),
-        name="final_sums",
-    )(grad_q, grad_k, grad_v, weights, rows_all, grad_one, ups_full, down_q_t, down_v_t)
+        name="final_sums_wide" if reach else "final_sums",
+    )(grad_q, grad_k, grad_v, far_rows, weights, grad_one, sums)
 
 
 def hand_out_kernel(grad_ref, sums_ref, grad_out, aq_ref, av_ref, bq_ref, bv_ref):
@@ -1260,7 +1423,7 @@
     token_rows = tokens.shape[0]
     down_q_t, down_v_t = query_down_factor.T, value_down_factor.T
     if fast:
-        full, weights, rows_all, q_own, k_all, v_all, ups_full = gather_all(
+        full, weights, rows_all, q_own, k_all, v_all, ups_full, fewest = gather_all(
             query_weight,
             w_key,
             value_weight,
@@ -1272,6 +1435,7 @@
             value_up_factor,
             down_q_t,
             down_v_t,
+            lengths,
         )
         full = full.reshape(2, 4, width, width)
     else:
@@ -1284,44 +1448,47 @@
         ups = jnp.pad(ups, ((0, 0), (0, -slim % 128)))
         ups_all = lax.all_gather(ups, "tensor")
         downs = jnp.concatenate([down_q_t, down_v_t], axis=0)
+        ups_full = ups_all[:, :, :slim].transpose(1, 0, 2).reshape(16, width)
         order = tuple(range(full.shape[1]))
         weights, q_own, k_all, v_all = project(order, full, rows_all, ups_all, downs, token_rows)
 
     norms = (gain_attn, shift_attn, gain_ffn, shift_ffn)
-    mixed, grad_one, grad_q, grad_k, grad_v = middle(
-        lengths, norms, q_own, k_all, v_all, tokens, cotangent, weights, full
+    mixed, grad_one, grad_q, grad_k, grad_v, far_rows, sums = middle(
+        lengths,
+        norms,
+        q_own,
+        k_all,
+        v_all,
+        tokens,
+        cotangent,
+        weights,
+        full,
+        rows_all,
+        ups_full,
+        (down_q_t, down_v_t),
     )
     if fast:
-        grad_tokens, sums = final_sums(
-            grad_q, grad_k, grad_v, weights, rows_all, grad_one, ups_full, down_q_t, down_v_t
+        operands = (grad_q, grad_k, grad_v, far_rows, weights, grad_one, sums)
+        grad_tokens, sums = lax.cond(
+            fewest[0, 0] >= rows_all.shape[0] // 2,
+            functools.partial(final_sums, False),
+            functools.partial(final_sums, True),
+            *operands,
         )
         grad_tokens, grad_aq, grad_av, grad_bq, grad_bv = hand_out(grad_tokens, sums, slim)
         return (mixed, grad_tokens, grad_aq.T, grad_bq, grad_av.T, grad_bv)
 
-    query_up = ups_all[:, :8, :slim].transpose(1, 0, 2).reshape(8, width)
-    value_up = ups_all[:, 8:, :slim].transpose(1, 0, 2).reshape(8, width)
-    w_q, w_k, w_v = weights[0], weights[1], weights[2]
-    u_query = dot_nn(tokens, query_down_factor).astype(jnp.bfloat16)
-    u_value = dot_nn(rows_all, value_down_factor).astype(jnp.bfloat16)
-    grad_uq = ADAPTER_SCALE * dot_nt(grad_q, query_up)
-    grad_uv = ADAPTER_SCALE * dot_nt(grad_v, value_up)
-    grad_bq = ADAPTER_SCALE * dot_tn(u_query, grad_q)
-    grad_bv = ADAPTER_SCALE * dot_tn(u_value, grad_v)
-    grad_aq = dot_tn(tokens, grad_uq.astype(jnp.bfloat16))
-    grad_av = dot_tn(rows_all, grad_uv.astype(jnp.bfloat16))
-    grad_rows = dot_nt(grad_k, w_k) + dot_nt(grad_v, w_v)
-    own_rows = dot_nt(grad_q, w_q)
+    grad_rows = dot_nt(grad_k, weights[1]) + dot_nt(grad_v, weights[2])
     shared = lax.psum_scatter(
         grad_rows.astype(jnp.bfloat16), "tensor", scatter_dimension=0, tiled=True
     )
+    own_rows = dot_nt(grad_q, weights[0])
     grad_tokens = (grad_one + own_rows + shared.astype(jnp.float32)).astype(jnp.bfloat16)
-    grad_aq, grad_av, grad_bq, grad_bv = lax.psum(
-        (grad_aq, grad_av, grad_bq, grad_bv), ("dp", "tensor")
-    )
+    sums = lax.psum(sums, ("dp", "tensor"))
     at = lax.axis_index("tensor") * slim
-    grad_bq = lax.dynamic_slice_in_dim(grad_bq, at, slim, 1)
-    grad_bv = lax.dynamic_slice_in_dim(grad_bv, at, slim, 1)
-    return (mixed, grad_tokens, grad_aq, grad_bq, grad_av, grad_bv)
+    grad_bq = lax.dynamic_slice_in_dim(sums[16:24], at, slim, 1)
+    grad_bv = lax.dynamic_slice_in_dim(sums[24:32], at, slim, 1)
+    return (mixed, grad_tokens, sums[0:8].T, grad_bq, sums[8:16].T, grad_bv)
 
 
 def solution(mesh):

time: 146 us -> 140 us (0.959)
  Pallas kernels: 145 us -> 138 us
    pallas_call x1, Pallas kernels: 28.4 us -> 17.7 us  [final_sums(): pl.pallas_call(functools.partial(final_kernel, reach), out_shape=(jax.Sha...]
    pallas_call x1, Pallas kernels: 42.5 us -> 45.2 us  [middle(): pl.pallas_call(middle_kernel, out_shape=(jax.ShapeDtypeStruct((rows, widt...]
where the time goes in v2:
time: 140 us
  Pallas kernels  138 us (99%)
    pallas_call x1, Pallas kernels, gather_all(): pl.pallas_call(gather_kernel, out_shape=(jax.ShapeDtypeStruct((2,) + grid...  73.2 us
    pallas_call x1, Pallas kernels, middle(): pl.pallas_call(middle_kernel, out_shape=(jax.ShapeDtypeStruct((rows, widt...  45.2 us
    pallas_call x1, Pallas kernels, final_sums(): pl.pallas_call(functools.partial(final_kernel, reach), out_shape=(jax.Sha...  17.7 us

profile of v2, /device:TPU:0, one launch (start us, length us, event | category | flops | bytes accessed | tf_op | source)
XLA Modules:
  0.0 139.6 jit_solution(4112734369643491008)
XLA Ops:
  0.6 73.2 %gather_all.1 = (bf16[2,2,2,4,2,96,768]{6,5,4,3,2,1,0:T(8,128)(2,1)}, bf16[4,768,768]{2,1,0:T(8,128)(2,1)}, bf16[2048,768]{1,0:T(8,128)(2,1)}, bf16[512,768]{1,0...) custom-call(bf16[96,192]{1,0:T(8,128)(2,1)} %wq_ref.1, ...), custom_call_target="tpu_custom_call" | custom-call | tf_op jit(solution)/shard_map/gather_all/pallas_call | solution.py:629
  74.4 45.2 %middle.1 = (bf16[512,768]{1,0:T(8,128)(2,1)}, f32[512,768]{1,0:T(8,128)}, bf16[512,768]{1,0:T(8,128)(2,1)S(1)}, bf16[2048,768]{1,0:T(8,128)(2,1)S(1)}, bf16[204...) custom-call(s32[1,32]{1,0:T(1,128)} %lengths_ref.3, f32[768]{0:T(1024)} %gain_attn_ref.1, ...), custom_call_target="tpu_custom_call" | custom-call | tf_op jit(solution)/shard_map/middle/pallas_call | solution.py:1030
  119.6 17.9 %conditional.1 = ((bf16[512,768]{1,0:T(8,128)(2,1)}, f32[32,768]{1,0:T(8,128)S(1)})) conditional(s32[]{:T(128)} %bitcast.4, (bf16[512,768]{1,0:T(8,128)(2,1)S(1)}, bf16[2048,768]{1,0:T(8,128)(2,1)S(1)}, bf16[2048,768]{1,0:T(8,128)(2,1)}, bf16[1024,768]{1,0:T(8,128)(2,1)}, bf16[4,768,768]{2,1,0:T(8,128)(2,1)}, /*index=5*/f32[512,768]{1,0:T(8,128)}, ...), branch_computations={%region_0.0_spmd, %region_1.0_spmd} | conditional | bytes 8 | solution.py:1472
  119.9 17.7 %final_sums.1 = (bf16[512,768]{1,0:T(8,128)(2,1)}, f32[32,768]{1,0:T(8,128)S(1)}) custom-call(bf16[512,768]{1,0:T(8,128)(2,1)S(1)} %get-tuple-element.35.gq_hbm, bf16[2048,768]{1,0:T(8,128)(2,1)S(1)} %get-tuple-element.36.gk_hbm, bf16[2048,768]{1,0:T(8,128)(2,1)} %get-tuple-element.37.gv_hbm, bf16[1024,768]{1,0:T(8,128)(2,1)} %get-tuple-element.38.far_hbm, ...), custom_call_target="tpu_custom_call" | custom-call | tf_op jit(solution)/shard_map/cond/branch_1_fun/final_sums/pallas_call | solution.py:1330
  137.5 2.1 %hand_out.1 = (bf16[512,768]{1,0:T(8,128)(2,1)}, f32[8,768]{1,0:T(8,128)}, f32[8,768]{1,0:T(8,128)}, f32[8,192]{1,0:T(8,128)}, f32[8,192]{1,0:T(8,128)}) custom-call(bf16[512,768]{1,0:T(8,128)(2,1)} %get-tuple-element.85.grad_ref, f32[32,768]{1,0:T(8,128)S(1)} %get-tuple-element.86.sums_ref), custom_call_target="tpu_custom_call" | custom-call | tf_op jit(solution)/shard_map/hand_out/pallas_call | solution.py:1386

commit v3 on v2

--- a/solution.py
+++ b/solution.py
@@ -13,8 +13,9 @@
 Q_BLOCK = 256
 K_BLOCK = 512
 KV_BLOCK = 256
+NORM_BLOCK = 512
 FAR_CHUNKS = 4
-FORWARD_GROUP = 3
+FORWARD_GROUP = 6
 BACKWARD_GROUP = 3
 ADAPTER_SCALE = 2.0
 SCORE_SCALE = HEAD_DIM ** (-0.5)
@@ -751,6 +752,7 @@
 
 
 def middle_kernel(
+    near_only,
     lengths_ref,
     gain_attn_ref,
     shift_attn_ref,
@@ -797,6 +799,7 @@
     far_out,
     pair_buf,
     sums_ref,
+    sums_low,
     load_sem,
     part_sem,
     kv_sem,
@@ -853,6 +856,17 @@
             for copy in kv_copies(block):
                 copy.start()
 
+    gk_acc[...] = jnp.zeros_like(gk_acc)
+    gv_acc[...] = jnp.zeros_like(gv_acc)
+    q_copy.wait()
+
+    @pl.loop(0, kv_blocks)
+    def _(block):
+        @pl.when(touched(block))
+        def _():
+            for copy in kv_copies(block):
+                copy.wait()
+
     tokens_copy.start()
     out_copy.start()
     cot_copy.start()
@@ -861,17 +875,6 @@
             copy.start()
     pair_copy.start()
 
-    gk_acc[...] = jnp.zeros_like(gk_acc)
-    gv_acc[...] = jnp.zeros_like(gv_acc)
-    q_copy.wait()
-
-    @pl.loop(0, kv_blocks)
-    def _(block):
-        @pl.when(touched(block))
-        def _():
-            for copy in kv_copies(block):
-                copy.wait()
-
     attend_forward(lengths_ref, q_ref, k_ref, v_ref, ctx_ref, lse_ref)
 
     gain_attn, shift_attn, gain_ffn, shift_ffn = (
@@ -879,12 +882,21 @@
     )
     tokens_copy.wait()
     out_copy.wait()
-    residual = tokens_ref[...].astype(jnp.float32) + dot_nt(ctx_ref[...], out_buf[...])
-    first, normed, inverse = norm_forward(residual, gain_attn, shift_attn)
-    first_buf[...] = first.astype(jnp.bfloat16)
-    sum_buf[...] = first.astype(jnp.bfloat16).astype(jnp.float32)
-    normed_buf[...] = normed
-    inverse_buf[...] = inverse
+    sum_buf[...] = dot_nt(ctx_ref[...], out_buf[...])
+
+    def each_norm_block(step):
+        @pl.loop(0, rows // NORM_BLOCK)
+        def _(at):
+            step(pl.ds(pl.multiple_of(at * NORM_BLOCK, NORM_BLOCK), NORM_BLOCK))
+
+    @each_norm_block
+    def _(block):
+        residual = tokens_ref[block, :].astype(jnp.float32) + sum_buf[block, :]
+        first, normed, inverse = norm_forward(residual, gain_attn, shift_attn)
+        first_buf[block, :] = first.astype(jnp.bfloat16)
+        sum_buf[block, :] = first.astype(jnp.bfloat16).astype(jnp.float32)
+        normed_buf[block, :] = normed
+        inverse_buf[block, :] = inverse
 
     @pl.loop(0, parts)
     def _(part):
@@ -895,24 +907,35 @@
         sum_buf[...] += dot_nt(acted.astype(jnp.bfloat16), down_buf[part])
 
     cot_copy.wait()
-    mixed, normed, inverse = norm_forward(sum_buf[...], gain_ffn, shift_ffn)
-    tokens_ref[...] = mixed.astype(jnp.bfloat16)
+
+    @each_norm_block
+    def _(block):
+        mixed, normed, inverse = norm_forward(sum_buf[block, :], gain_ffn, shift_ffn)
+        tokens_ref[block, :] = mixed.astype(jnp.bfloat16)
+        cotangents = cot_ref[block, :].astype(jnp.float32)
+        grad_two = norm_backward(cotangents, normed, inverse, gain_ffn)
+        first_buf[block, :] = grad_two.astype(jnp.bfloat16)
+        sum_buf[block, :] = grad_two
+
     mixed_copy = pltpu.make_async_copy(tokens_ref, mixed_hbm, store_sem.at[0])
     mixed_copy.start()
-    grad_two = norm_backward(cot_ref[...].astype(jnp.float32), normed, inverse, gain_ffn)
-    first_buf[...] = grad_two.astype(jnp.bfloat16)
-    sum_buf[...] = grad_two
 
     @pl.loop(0, parts)
     def _(part):
         grad_hidden = dot_nn(first_buf[...], down_buf[part]) * slope_buf[part]
         sum_buf[...] += dot_nt(grad_hidden.astype(jnp.bfloat16), in_buf[part])
 
-    grad_one = norm_backward(sum_buf[...], normed_buf[...], inverse_buf[...], gain_attn)
-    normed_buf[...] = grad_one
+    @each_norm_block
+    def _(block):
+        grad_one = norm_backward(
+            sum_buf[block, :], normed_buf[block, :], inverse_buf[block, :], gain_attn
+        )
+        normed_buf[block, :] = grad_one
+        first_buf[block, :] = grad_one.astype(jnp.bfloat16)
+
     grad_one_copy = pltpu.make_async_copy(normed_buf, grad_one_hbm, store_sem.at[1])
     grad_one_copy.start()
-    grad_ref[...] = dot_nn(grad_one.astype(jnp.bfloat16), out_buf[...]).astype(jnp.bfloat16)
+    grad_ref[...] = dot_nn(first_buf[...], out_buf[...]).astype(jnp.bfloat16)
 
     attend_backward(
         lengths_ref, q_ref, k_ref, v_ref, ctx_ref, lse_ref, grad_ref, first_buf, gk_acc, gv_acc
@@ -929,6 +952,11 @@
         @pl.when(touched(block))
         def _():
             rows_copy(block).start()
+
+    def wanted(block):
+        if not near_only:
+            return block >= 0
+        return block // (kv_blocks // 2) == lax.axis_index("tensor") // 2
 
     def grad_copies(block):
         window = kv_rows(block)
@@ -951,8 +979,10 @@
             gk_out[window, :] = jnp.zeros((KV_BLOCK, width), jnp.bfloat16)
             gv_out[window, :] = jnp.zeros((KV_BLOCK, width), jnp.bfloat16)
 
-        for copy in grad_copies(block):
-            copy.start()
+        @pl.when(wanted(block))
+        def _():
+            for copy in grad_copies(block):
+                copy.start()
 
     def far_copy(at):
         window = kv_rows(at)
@@ -1000,7 +1030,8 @@
 
     own = pl.ds(pl.multiple_of(base, rows), rows)
     add_adapter(k_ref[own, :], first_buf[...], down_q_ref[...], ups_ref[0:8, :], 0, 16)
-    sums_copy = pltpu.make_async_copy(sums_ref, sums_hbm, store_sem.at[3])
+    sums_low[...] = sums_ref[...].astype(jnp.bfloat16)
+    sums_copy = pltpu.make_async_copy(sums_low, sums_hbm, store_sem.at[3])
     sums_copy.start()
     sums_copy.wait()
 
@@ -1013,12 +1044,14 @@
 
     @pl.loop(0, kv_blocks)
     def _(block):
-        for copy in grad_copies(block):
-            copy.wait()
+        @pl.when(wanted(block))
+        def _():
+            for copy in grad_copies(block):
+                copy.wait()
 
 
 def middle(
-    lengths, norms, q_own, k_all, v_all, tokens, cotangent, weights, full, rows_all, ups, downs
+    near_only, lengths, norms, q_own, k_all, v_all, tokens, cotangent, weights, full, rows_all, ups, downs
 ):
     rows, width = q_own.shape
     total_rows = k_all.shape[0]
@@ -1028,7 +1061,7 @@
     kv_blocks = total_rows // KV_BLOCK
     dma = pltpu.SemaphoreType.DMA
     return pl.pallas_call(
-        middle_kernel,
+        functools.partial(middle_kernel, near_only),
         out_shape=(
             jax.ShapeDtypeStruct((rows, width), bf16),
             jax.ShapeDtypeStruct((rows, width), f32),
@@ -1036,7 +1069,7 @@
             jax.ShapeDtypeStruct((total_rows, width), bf16),
             jax.ShapeDtypeStruct((total_rows, width), bf16),
             jax.ShapeDtypeStruct((total_rows // 2, width), bf16),
-            jax.ShapeDtypeStruct((32, width), f32),
+            jax.ShapeDtypeStruct((32, width), bf16),
         ),
         in_specs=[SMEM_SPEC] + [VMEM_SPEC] * 4 + [HBM_SPEC] * 8 + [VMEM_SPEC] * 3,
         out_specs=(HBM_SPEC,) * 7,
@@ -1064,6 +1097,7 @@
             pltpu.VMEM((total_rows // 2, width), bf16),
             pltpu.VMEM((2, width, width), bf16),
             pltpu.VMEM((32, width), f32),
+            pltpu.VMEM((32, width), bf16),
             dma((5,)),
             dma((2, parts)),
             dma((2, kv_blocks)),
@@ -1111,12 +1145,9 @@
     from_x,
     home_to,
     home_from,
-    sums_in,
-    total,
-    total_in,
-    step_out,
-    step_in,
+    yc_slots,
     z_slots,
+    xc_slots,
     load_sem,
     far_send,
     far_recv,
@@ -1150,19 +1181,12 @@
     across = place.device(x=1 - x, core=1 - core)
     middle_device = x != core
     barrier = pltpu.get_barrier_semaphore()
-    others = [place.sibling(), place.step("x", 1), place.step("y", 1)]
-    others += [place.device(z=lax.rem(z + i, DEPTH)) for i in range(1, DEPTH)]
-    for target in others:
+    around = [place.step("y", 1), place.sibling(), place.device(y=1 - y, core=1 - core)]
+    column = [place.device(z=lax.rem(z + i, DEPTH)) for i in range(1, DEPTH)]
+    beside = [place.step("x", 1), across]
+    for target in around + column + beside:
         pl.semaphore_signal(barrier, inc=1, device_id=target, device_id_type=MESH_ID)
-    greeted = len(others)
-    if not reach:
-
-        @pl.when(middle_device)
-        def _():
-            pl.semaphore_signal(barrier, inc=1, device_id=across, device_id_type=MESH_ID)
-
-        greeted = greeted + middle_device.astype(jnp.int32)
-    pl.semaphore_wait(barrier, greeted)
+    pl.semaphore_wait(barrier, len(around + column + beside))
 
     def remote(source, target, send, recv, device):
         return pltpu.make_async_remote_copy(
@@ -1182,9 +1206,15 @@
     chunks = [pl.ds(at * chunk_rows, chunk_rows) for at in range(FAR_CHUNKS)]
     kept = pl.ds(pl.multiple_of(core * 16, 16), 16)
     given = pl.ds(pl.multiple_of((1 - core) * 16, 16), 16)
-    sum_copies = [
-        started(part_sums.at[given], sums_in, sum_send.at[0], sum_recv.at[0], place.sibling())
-    ]
+    sum_copies = []
+
+    def send_sum(source, target, device):
+        at = len(sum_copies)
+        sum_copies.append(started(source, target, sum_send.at[at], sum_recv.at[at], device))
+
+    for source, device in zip((kept, given, given), around):
+        send_sum(part_sums.at[source], yc_slots.at[y * 2 + core], device)
+    yc_slots[y * 2 + core] = part_sums[kept, :]
     sib_copies, x_copies = [], []
     if reach:
         for at, chunk in enumerate(chunks):
@@ -1218,11 +1248,12 @@
         def _():
             from_x[...] = jnp.zeros_like(from_x)
 
-    sum_copies[0].wait_recv()
-    step_out[0] = (part_sums[kept, :] + sums_in[...]).astype(bf16)
-    sum_copies.append(
-        started(step_out.at[0], step_in.at[0], sum_send.at[1], sum_recv.at[1], place.step("y", 1))
-    )
+    def slot_sum(slots, indices):
+        result = slots[indices[0]].astype(f32)
+        for i in indices[1:]:
+            result = result + slots[i].astype(f32)
+        return result
+
     if reach:
         loads["far"].wait()
         for at, chunk in enumerate(chunks):
@@ -1240,18 +1271,11 @@
                 )
             )
 
-    sum_copies[1].wait_recv()
-    z_slots[z] = (step_out[0].astype(f32) + step_in[0].astype(f32)).astype(bf16)
-    for i in range(1, DEPTH):
-        sum_copies.append(
-            started(
-                z_slots.at[z],
-                z_slots.at[z],
-                sum_send.at[1 + i],
-                sum_recv.at[1 + i],
-                place.device(z=lax.rem(z + i, DEPTH)),
-            )
-        )
+    for copy in sum_copies[0:3]:
+        copy.wait_recv()
+    z_slots[z] = slot_sum(yc_slots, range(4)).astype(bf16)
+    for device in column:
+        send_sum(z_slots.at[z], z_slots.at[z], device)
 
     def partial(owner, half):
         window = pl.ds(pl.multiple_of(owner * token_rows + half * half_rows, half_rows), half_rows)
@@ -1273,32 +1297,17 @@
             )
         )
 
-    for i in range(1, DEPTH):
-        sum_copies[1 + i].wait_recv()
-    column = z_slots[0].astype(f32)
-    for i in range(1, DEPTH):
-        column = column + z_slots[i].astype(f32)
-    step_out[1] = column.astype(bf16)
-    sum_copies.append(
-        started(
-            step_out.at[1],
-            step_in.at[1],
-            sum_send.at[DEPTH + 1],
-            sum_recv.at[DEPTH + 1],
-            place.step("x", 1),
-        )
-    )
+    for copy in sum_copies[3:]:
+        copy.wait_recv()
+    xc_slots[x * 2 + core] = slot_sum(z_slots, range(DEPTH)).astype(bf16)
+    own_slot = xc_slots.at[x * 2 + core]
+    for device in [place.sibling()] + beside:
+        send_sum(own_slot, own_slot, device)
     for name in ("q", "one"):
         loads[name].wait()
     for half in range(2):
         window = pl.ds(half * half_rows, half_rows)
         grad_one_ref[window, :] += partial(core, half) + dot_nt(gq_ref[window, :], weights_ref[0])
-    sum_copies[-1].wait_recv()
-    total[...] = step_out[1].astype(f32) + step_in[1].astype(f32)
-    sum_copies.append(
-        started(total, total_in, sum_send.at[DEPTH + 2], sum_recv.at[DEPTH + 2], place.sibling())
-    )
-
     for copy in home_copies:
         copy.wait_recv()
     for at, chunk in enumerate(chunks):
@@ -1309,9 +1318,10 @@
         grad_tokens_ref[chunk, :] = (
             grad_one_ref[chunk, :] + home_from[chunk, :].astype(f32) + from_x[chunk, :].astype(f32)
         ).astype(bf16)
-    sum_copies[-1].wait_recv()
-    sums_ref[kept, :] = total[...]
-    sums_ref[given, :] = total_in[...]
+    for copy in sum_copies[2 + DEPTH :]:
+        copy.wait_recv()
+    for half in range(2):
+        sums_ref[half * 16 : half * 16 + 16, :] = slot_sum(xc_slots, (half, 2 + half))
 
     for copy in sib_copies + home_copies + sum_copies:
         copy.wait_send()
@@ -1347,19 +1357,16 @@
             block,
             block,
             block,
-            pltpu.VMEM((16, width), f32),
-            pltpu.VMEM((16, width), f32),
-            pltpu.VMEM((16, width), f32),
-            pltpu.VMEM((2, 16, width), bf16),
-            pltpu.VMEM((2, 16, width), bf16),
+            pltpu.VMEM((4, 16, width), bf16),
             pltpu.VMEM((DEPTH, 16, width), bf16),
+            pltpu.VMEM((4, 16, width), bf16),
             dma((6,)),
             dma((2, FAR_CHUNKS)),
             dma((2, FAR_CHUNKS)),
             dma((2,)),
             dma((2,)),
-            dma((DEPTH + 3,)),
-            dma((DEPTH + 3,)),
+            dma((DEPTH + 5,)),
+            dma((DEPTH + 5,)),
         ],
         compiler_params=pltpu.CompilerParams(
             collective_id=2 if reach else 3, has_side_effects=True, vmem_limit_bytes=VMEM_LIMIT
@@ -1454,6 +1461,7 @@
 
     norms = (gain_attn, shift_attn, gain_ffn, shift_ffn)
     mixed, grad_one, grad_q, grad_k, grad_v, far_rows, sums = middle(
+        fast,
         lengths,
         norms,
         q_own,
@@ -1484,7 +1492,7 @@
     )
     own_rows = dot_nt(grad_q, weights[0])
     grad_tokens = (grad_one + own_rows + shared.astype(jnp.float32)).astype(jnp.bfloat16)
-    sums = lax.psum(sums, ("dp", "tensor"))
+    sums = lax.psum(sums.astype(jnp.float32), ("dp", "tensor"))
     at = lax.axis_index("tensor") * slim
     grad_bq = lax.dynamic_slice_in_dim(sums[16:24], at, slim, 1)
     grad_bv = lax.dynamic_slice_in_dim(sums[24:32], at, slim, 1)

time: 140 us -> 138 us (0.986)
    pallas_call x1, Pallas kernels: 45.2 us -> 43.3 us  [middle(): pl.pallas_call(functools.partial(middle_kernel, near_only), out_shape=(ja...]
where the time goes in v3:
time: 138 us
  Pallas kernels  137 us (99%)
    pallas_call x1, Pallas kernels, gather_all(): pl.pallas_call(gather_kernel, out_shape=(jax.ShapeDtypeStruct((2,) + grid...  73.2 us
    pallas_call x1, Pallas kernels, middle(): pl.pallas_call(functools.partial(middle_kernel, near_only), out_shape=(ja...  43.3 us
    pallas_call x1, Pallas kernels, final_sums(): pl.pallas_call(functools.partial(final_kernel, reach), out_shape=(jax.Sha...  18 us

profile of v3, /device:TPU:0, one launch (start us, length us, event | category | flops | bytes accessed | tf_op | source)
XLA Modules:
  0.0 137.9 jit_solution(7485303822344452301)
XLA Ops:
  0.6 73.2 %gather_all.1 = (bf16[2,2,2,4,2,96,768]{6,5,4,3,2,1,0:T(8,128)(2,1)}, bf16[4,768,768]{2,1,0:T(8,128)(2,1)}, bf16[2048,768]{1,0:T(8,128)(2,1)}, bf16[512,768]{1,0...) custom-call(bf16[96,192]{1,0:T(8,128)(2,1)} %wq_ref.1, ...), custom_call_target="tpu_custom_call" | custom-call | tf_op jit(solution)/shard_map/gather_all/pallas_call | solution.py:630
  74.4 43.3 %middle.1 = (bf16[512,768]{1,0:T(8,128)(2,1)}, f32[512,768]{1,0:T(8,128)}, bf16[512,768]{1,0:T(8,128)(2,1)S(1)}, bf16[2048,768]{1,0:T(8,128)(2,1)S(1)}, bf16[204...) custom-call(s32[1,32]{1,0:T(1,128)} %lengths_ref.3, f32[768]{0:T(1024)} %gain_attn_ref.1, ...), custom_call_target="tpu_custom_call" | custom-call | tf_op jit(solution)/shard_map/middle/pallas_call | solution.py:1063
  117.8 18.0 %conditional.1 = ((bf16[512,768]{1,0:T(8,128)(2,1)}, f32[32,768]{1,0:T(8,128)S(1)})) conditional(s32[]{:T(128)} %bitcast.4, (bf16[512,768]{1,0:T(8,128)(2,1)S(1)}, bf16[2048,768]{1,0:T(8,128)(2,1)S(1)}, bf16[2048,768]{1,0:T(8,128)(2,1)}, bf16[1024,768]{1,0:T(8,128)(2,1)}, bf16[4,768,768]{2,1,0:T(8,128)(2,1)}, /*index=5*/f32[512,768]{1,0:T(8,128)}, ...), branch_computations={%region_0.0_spmd, %region_1.0_spmd} | conditional | bytes 8 | solution.py:1480
  117.8 18.0 %final_sums.1 = (bf16[512,768]{1,0:T(8,128)(2,1)}, f32[32,768]{1,0:T(8,128)S(1)}) custom-call(bf16[512,768]{1,0:T(8,128)(2,1)S(1)} %get-tuple-element.35.gq_hbm, bf16[2048,768]{1,0:T(8,128)(2,1)S(1)} %get-tuple-element.36.gk_hbm, bf16[2048,768]{1,0:T(8,128)(2,1)} %get-tuple-element.37.gv_hbm, bf16[1024,768]{1,0:T(8,128)(2,1)} %get-tuple-element.38.far_hbm, ...), custom_call_target="tpu_custom_call" | custom-call | tf_op jit(solution)/shard_map/cond/branch_1_fun/final_sums/pallas_call | solution.py:1340
  135.8 2.1 %hand_out.1 = (bf16[512,768]{1,0:T(8,128)(2,1)}, f32[8,768]{1,0:T(8,128)}, f32[8,768]{1,0:T(8,128)}, f32[8,192]{1,0:T(8,128)}, f32[8,192]{1,0:T(8,128)}) custom-call(bf16[512,768]{1,0:T(8,128)(2,1)} %get-tuple-element.85.grad_ref, f32[32,768]{1,0:T(8,128)S(1)} %get-tuple-element.86.sums_ref), custom_call_target="tpu_custom_call" | custom-call | tf_op jit(solution)/shard_map/hand_out/pallas_call | solution.py:1393

commit v4 on v3

--- a/solution.py
+++ b/solution.py
@@ -113,9 +113,9 @@
     return joined.T
 
 
-def window_mask(step, low, begin, finish, total_rows):
+def window_mask(step, low, begin, finish, limit):
     wanted = low + step * K_BLOCK
-    start = pl.multiple_of(jnp.minimum(wanted, total_rows - K_BLOCK), 16)
+    start = pl.multiple_of(jnp.minimum(wanted, limit - K_BLOCK), 16)
     key_at = start + lax.broadcasted_iota(jnp.int32, (K_BLOCK, begin.shape[1]), 0)
     return start, (key_at >= jnp.maximum(begin, wanted)) & (key_at < finish)
 
@@ -144,14 +144,14 @@
             block_step(q_rows, lanes, slots, low, steps, begin, finish)
 
 
-def attend_forward(lengths_ref, q_ref, k_ref, v_ref, out_ref, lse_ref):
+def attend_forward(limit, lengths_ref, q_ref, k_ref, v_ref, out_ref, lse_ref):
     total_rows = k_ref.shape[0]
 
     def block_step(q_rows, lanes, slots, low, steps, begin, finish):
         q_two = [stack_pair(q_ref[q_rows, lane]) for lane in lanes]
 
         def body(step, carry):
-            start, allowed = window_mask(step, low, begin, finish, total_rows)
+            start, allowed = window_mask(step, low, begin, finish, limit)
             window = pl.ds(start, K_BLOCK)
             both = jnp.concatenate([allowed, allowed], axis=1)
             result = []
@@ -181,7 +181,7 @@
 
 
 def attend_backward(
-    lengths_ref, q_ref, k_ref, v_ref, ctx_ref, lse_ref, grad_ref, gq_ref, gk_acc, gv_acc
+    limit, lengths_ref, q_ref, k_ref, v_ref, ctx_ref, lse_ref, grad_ref, gq_ref, gk_acc, gv_acc
 ):
     total_rows = k_ref.shape[0]
 
@@ -200,7 +200,7 @@
             ready.append((stack_pair(q_ref[q_rows, lane]), stack_pair(grads), row_dot, lse_ref[slot]))
 
         def body(step, carry):
-            start, allowed = window_mask(step, low, begin, finish, total_rows)
+            start, allowed = window_mask(step, low, begin, finish, limit)
             window = pl.ds(start, K_BLOCK)
             both = jnp.concatenate([allowed, allowed], axis=1)
             result = []
@@ -351,6 +351,7 @@
     ups_send,
     ups_recv,
     out_sem,
+    far_sem,
 ):
     place = Place()
     x, y, z, core = place.x, place.y, place.z, place.core
@@ -358,11 +359,13 @@
     part_rows = FULL_ROWS // 2
     half_rows = token_rows // 2
 
+    across = place.device(x=1 - x, core=1 - core)
+    middle_device = x != core
     barrier = pltpu.get_barrier_semaphore()
     others = (
         place.sibling(),
         place.step("x", 1),
-        place.device(x=1 - x, core=1 - core),
+        across,
         place.step("y", 1),
     )
     for target in others:
@@ -407,7 +410,7 @@
     row_copies = []
     for half in range(2):
         source = tokens_ref.at[pl.ds(half * half_rows, half_rows)]
-        for slot, device in ((0, place.step("x", 1)), (1, place.sibling())):
+        for slot, device in ((0, across), (1, place.sibling())):
             row_copies.append(
                 remote(
                     source,
@@ -505,8 +508,17 @@
                             block, block, send_sem.at[flow, slot], sib_recv.at[flow], place.sibling()
                         ).wait_send()
 
-    for copy in row_copies + up_copies + own_copies:
+    across_copies, sibling_copies = row_copies[0::2], row_copies[1::2]
+    for copy in sibling_copies + up_copies + own_copies:
         copy.start()
+
+    def middle_devices(step):
+        pl.when(middle_device)(step)
+
+    @middle_devices
+    def _():
+        for copy in across_copies:
+            copy.start()
 
     count_copies = [
         remote(
@@ -525,29 +537,43 @@
             copy.start()
             count_copies.append(copy)
 
-    def pass_rows(half):
-        row_copies[2 * half].wait_recv()
-        landed = rows_at(1 - x, core, half)
-        copy = remote(landed, landed, rows_send.at[2, half], rows_recv.at[2, half], place.sibling())
-        copy.start()
-        return copy
-
     outs = []
+
+    far_owner = (1 - x) * 2 + 1 - core
+    far_writes = []
 
     def write(source, target):
         copy = pltpu.make_async_copy(source, target, out_sem.at[len(outs)])
         copy.start()
         outs.append(copy)
 
+    def block_of_rows(hbm, owner):
+        return hbm.at[pl.ds(pl.multiple_of(owner * token_rows, token_rows), token_rows)]
+
+    def write_rows(source, hbm, owner):
+        write(source, block_of_rows(hbm, owner))
+
+    def far_write(source, hbm):
+        return pltpu.make_async_copy(
+            source, block_of_rows(hbm, far_owner), far_sem.at[len(far_writes)]
+        )
+
     def assemble(t):
         if t == 0:
             for copy in up_copies + own_copies[:3]:
                 copy.wait()
-            for half in range(2):
-                row_copies[2 * half + 1].wait_recv()
-                passed_rows[half].wait_recv()
-            for owner in range(4):
-                write(rows_ref.at[owner], rows_hbm.at[pl.ds(owner * token_rows, token_rows)])
+            for copy in sibling_copies:
+                copy.wait_recv()
+            for at in range(2):
+                write_rows(rows_ref.at[x * 2 + at], rows_hbm, x * 2 + at)
+            far_writes.append(far_write(rows_ref.at[far_owner], rows_hbm))
+
+            @middle_devices
+            def _():
+                for copy in across_copies:
+                    copy.wait_recv()
+                far_writes[0].start()
+
             finish_flow(0)
             finish_flow(1)
             for owner in range(4):
@@ -568,17 +594,28 @@
         q_ref[...] = dot_nn(rows_ref[x * 2 + core], weights_ref[0]).astype(jnp.bfloat16)
         write(q_ref, q_hbm)
 
-    def keys_values(ref, hbm, kind, owner):
-        ref[owner] = dot_nn(rows_ref[owner], weights_ref[kind]).astype(jnp.bfloat16)
-        write(ref.at[owner], hbm.at[pl.ds(owner * token_rows, token_rows)])
+    def keys_values(ref, hbm, kind, at):
+        owner = x * 2 + at
+        ref[at] = dot_nn(rows_ref[owner], weights_ref[kind]).astype(jnp.bfloat16)
+        write_rows(ref.at[at], hbm, owner)
+
+    def far_keys_values(ref, hbm, kind):
+        far_writes.append(far_write(ref.at[2], hbm))
+        at = len(far_writes) - 1
+
+        @middle_devices
+        def _():
+            ref[2] = dot_nn(rows_ref[far_owner], weights_ref[kind]).astype(jnp.bfloat16)
+            far_writes[at].start()
 
     steps = [functools.partial(assemble, t) for t in range(4)] + [own_queries]
-    for owner in range(4):
-        steps.append(functools.partial(keys_values, k_ref, k_hbm, 1, owner))
-        steps.append(functools.partial(keys_values, v_ref, v_hbm, 2, owner))
-
-    passed_rows = []
-    events = event_order(17.0)
+    for at in range(2):
+        steps.append(functools.partial(keys_values, k_ref, k_hbm, 1, at))
+        steps.append(functools.partial(keys_values, v_ref, v_hbm, 2, at))
+    steps.append(functools.partial(far_keys_values, k_ref, k_hbm, 1))
+    steps.append(functools.partial(far_keys_values, v_ref, v_hbm, 2))
+
+    events = event_order(8.5)
     last_pack = max(i for i, (flow, _) in enumerate(events) if FLOWS[flow][0] == 0)
     between = max(1, (len(events) - last_pack) // (len(steps) + 1))
     arrivals = 0
@@ -591,8 +628,6 @@
             )
         if piece != OWN:
             arrivals += 1
-            if arrivals in (8, 16):
-                passed_rows.append(pass_rows(len(passed_rows)))
             if arrivals == 24:
                 pass_count()
         if at >= last_pack and (at - last_pack) % between == between - 1 and steps:
@@ -600,10 +635,16 @@
     for step in steps:
         step()
 
-    for half in range(2):
-        row_copies[2 * half].wait_send()
-        row_copies[2 * half + 1].wait_send()
-        passed_rows[half].wait_send()
+    for copy in sibling_copies:
+        copy.wait_send()
+
+    @middle_devices
+    def _():
+        for copy in across_copies:
+            copy.wait_send()
+        for copy in far_writes:
+            copy.wait()
+
     for copy in own_copies[3:] + outs:
         copy.wait()
     for flow in range(len(FLOWS)):
@@ -649,8 +690,8 @@
             pltpu.VMEM((4, 16, padded), f32),
             pltpu.VMEM((4, width, width), bf16),
             pltpu.VMEM((token_rows, width), bf16),
-            pltpu.VMEM((4, token_rows, width), bf16),
-            pltpu.VMEM((4, token_rows, width), bf16),
+            pltpu.VMEM((3, token_rows, width), bf16),
+            pltpu.VMEM((3, token_rows, width), bf16),
             pltpu.VMEM((8, 128), f32),
             pltpu.VMEM((DEPTH + 1, 8, 128), f32),
             dma((DEPTH,)),
@@ -665,6 +706,7 @@
             dma((3,)),
             dma((3,)),
             dma((14,)),
+            dma((3,)),
         ],
         compiler_params=pltpu.CompilerParams(
             collective_id=1, has_side_effects=True, vmem_limit_bytes=VMEM_LIMIT
@@ -754,6 +796,7 @@
 def middle_kernel(
     near_only,
     lengths_ref,
+    fewest_ref,
     gain_attn_ref,
     shift_attn_ref,
     gain_ffn_ref,
@@ -766,6 +809,9 @@
     weights_hbm,
     full_hbm,
     rows_hbm,
+    wide_k_hbm,
+    wide_v_hbm,
+    wide_rows_hbm,
     ups_ref,
     down_q_ref,
     down_v_ref,
@@ -812,12 +858,14 @@
     parts, kinds = in_buf.shape[0], full_hbm.shape[0]
     kv_blocks = total_rows // KV_BLOCK
     base = lax.axis_index("tensor") * rows
+    wide = fewest_ref[0, 0] < total_rows // 2
+    limit = jnp.where(wide, total_rows, jnp.minimum(base + 2 * rows, total_rows))
 
     span_low, span_high = jnp.int32(total_rows), jnp.int32(0)
     for at in range(rows // Q_BLOCK):
         low, steps = query_span(lengths_ref, base + at * Q_BLOCK, total_rows)
-        span_low = jnp.minimum(span_low, jnp.minimum(low, total_rows - K_BLOCK))
-        span_high = jnp.maximum(span_high, jnp.minimum(low + steps * K_BLOCK, total_rows))
+        span_low = jnp.minimum(span_low, jnp.minimum(low, limit - K_BLOCK))
+        span_high = jnp.maximum(span_high, jnp.minimum(low + steps * K_BLOCK, limit))
 
     def kv_rows(block):
         return pl.ds(pl.multiple_of(block * KV_BLOCK, KV_BLOCK), KV_BLOCK)
@@ -825,11 +873,11 @@
     def touched(block):
         return (block * KV_BLOCK < span_high) & ((block + 1) * KV_BLOCK > span_low)
 
-    def kv_copies(block):
+    def kv_copies(block, k_source=k_hbm, v_source=v_hbm):
         window = kv_rows(block)
         return (
-            pltpu.make_async_copy(k_hbm.at[window], k_ref.at[window], kv_sem.at[0, block]),
-            pltpu.make_async_copy(v_hbm.at[window], v_ref.at[window], kv_sem.at[1, block]),
+            pltpu.make_async_copy(k_source.at[window], k_ref.at[window], kv_sem.at[0, block]),
+            pltpu.make_async_copy(v_source.at[window], v_ref.at[window], kv_sem.at[1, block]),
         )
 
     def part_copies(part):
@@ -851,9 +899,14 @@
 
     @pl.loop(0, kv_blocks)
     def _(block):
-        @pl.when(touched(block))
+        @pl.when(touched(block) & jnp.logical_not(wide))
         def _():
             for copy in kv_copies(block):
+                copy.start()
+
+        @pl.when(touched(block) & wide)
+        def _():
+            for copy in kv_copies(block, wide_k_hbm, wide_v_hbm):
                 copy.start()
 
     gk_acc[...] = jnp.zeros_like(gk_acc)
@@ -875,7 +928,7 @@
             copy.start()
     pair_copy.start()
 
-    attend_forward(lengths_ref, q_ref, k_ref, v_ref, ctx_ref, lse_ref)
+    attend_forward(limit, lengths_ref, q_ref, k_ref, v_ref, ctx_ref, lse_ref)
 
     gain_attn, shift_attn, gain_ffn, shift_ffn = (
         ref[...].reshape(1, -1) for ref in (gain_attn_ref, shift_attn_ref, gain_ffn_ref, shift_ffn_ref)
@@ -938,20 +991,34 @@
     grad_ref[...] = dot_nn(first_buf[...], out_buf[...]).astype(jnp.bfloat16)
 
     attend_backward(
-        lengths_ref, q_ref, k_ref, v_ref, ctx_ref, lse_ref, grad_ref, first_buf, gk_acc, gv_acc
+        limit,
+        lengths_ref,
+        q_ref,
+        k_ref,
+        v_ref,
+        ctx_ref,
+        lse_ref,
+        grad_ref,
+        first_buf,
+        gk_acc,
+        gv_acc,
     )
     gq_copy = pltpu.make_async_copy(first_buf, gq_hbm, store_sem.at[2])
     gq_copy.start()
 
-    def rows_copy(block):
+    def rows_copy(block, source=rows_hbm):
         window = kv_rows(block)
-        return pltpu.make_async_copy(rows_hbm.at[window], k_ref.at[window], kv_sem.at[0, block])
+        return pltpu.make_async_copy(source.at[window], k_ref.at[window], kv_sem.at[0, block])
 
     @pl.loop(0, kv_blocks)
     def _(block):
-        @pl.when(touched(block))
+        @pl.when(touched(block) & jnp.logical_not(wide))
         def _():
             rows_copy(block).start()
+
+        @pl.when(touched(block) & wide)
+        def _():
+            rows_copy(block, wide_rows_hbm).start()
 
     def wanted(block):
         if not near_only:
@@ -1051,7 +1118,21 @@
 
 
 def middle(
-    near_only, lengths, norms, q_own, k_all, v_all, tokens, cotangent, weights, full, rows_all, ups, downs
+    near_only,
+    lengths,
+    fewest,
+    norms,
+    q_own,
+    k_all,
+    v_all,
+    wide_rows,
+    tokens,
+    cotangent,
+    weights,
+    full,
+    rows_all,
+    ups,
+    downs,
 ):
     rows, width = q_own.shape
     total_rows = k_all.shape[0]
@@ -1071,7 +1152,7 @@
             jax.ShapeDtypeStruct((total_rows // 2, width), bf16),
             jax.ShapeDtypeStruct((32, width), bf16),
         ),
-        in_specs=[SMEM_SPEC] + [VMEM_SPEC] * 4 + [HBM_SPEC] * 8 + [VMEM_SPEC] * 3,
+        in_specs=[SMEM_SPEC] * 2 + [VMEM_SPEC] * 4 + [HBM_SPEC] * 11 + [VMEM_SPEC] * 3,
         out_specs=(HBM_SPEC,) * 7,
         scratch_shapes=[
             pltpu.VMEM((rows, width), bf16),
@@ -1109,6 +1190,7 @@
         name="middle",
     )(
         lengths,
+        fewest,
         *norms,
         q_own,
         k_all,
@@ -1118,6 +1200,7 @@
         weights,
         full,
         rows_all,
+        *wide_rows,
         ups,
         *downs,
     )
@@ -1373,6 +1456,17 @@
         ),
         name="final_sums_wide" if reach else "final_sums",
     )(grad_q, grad_k, grad_v, far_rows, weights, grad_one, sums)
+
+
+def no_rows_kernel(*refs):
+    del refs
+
+
+def no_rows(tokens, weights):
+    shape = jax.ShapeDtypeStruct((4 * tokens.shape[0], tokens.shape[1]), tokens.dtype)
+    return pl.pallas_call(
+        no_rows_kernel, out_shape=(shape,) * 3, out_specs=(HBM_SPEC,) * 3, name="no_rows"
+    )()
 
 
 def hand_out_kernel(grad_ref, sums_ref, grad_out, aq_ref, av_ref, bq_ref, bv_ref):
@@ -1460,32 +1554,67 @@
         weights, q_own, k_all, v_all = project(order, full, rows_all, ups_all, downs, token_rows)
 
     norms = (gain_attn, shift_attn, gain_ffn, shift_ffn)
+    downs_t = (down_q_t, down_v_t)
+    if fast:
+
+        def either(near, wide, *operands):
+            return lax.cond(fewest[0, 0] >= rows_all.shape[0] // 2, near, wide, *operands)
+
+        def wide_rows(tokens, weights):
+            me = lax.axis_index("tensor")
+            rows_all = jnp.zeros((4 * token_rows, width), tokens.dtype)
+            for away in range(4):
+                block = tokens
+                if away:
+                    block = lax.ppermute(tokens, "tensor", [(i, i ^ away) for i in range(4)])
+                first_row = (me ^ away) * token_rows
+                rows_all = lax.dynamic_update_slice_in_dim(rows_all, block, first_row, 0)
+            k_all = dot_nn(rows_all, weights[1]).astype(jnp.bfloat16)
+            v_all = dot_nn(rows_all, weights[2]).astype(jnp.bfloat16)
+            return (k_all, v_all, rows_all)
+
+        mixed, grad_one, grad_q, grad_k, grad_v, far_rows, sums = middle(
+            True,
+            lengths,
+            fewest,
+            norms,
+            q_own,
+            k_all,
+            v_all,
+            either(no_rows, wide_rows, tokens, weights),
+            tokens,
+            cotangent,
+            weights,
+            full,
+            rows_all,
+            ups_full,
+            downs_t,
+        )
+        grad_tokens, sums = either(
+            functools.partial(final_sums, False),
+            functools.partial(final_sums, True),
+            *(grad_q, grad_k, grad_v, far_rows, weights, grad_one, sums),
+        )
+        grad_tokens, grad_aq, grad_av, grad_bq, grad_bv = hand_out(grad_tokens, sums, slim)
+        return (mixed, grad_tokens, grad_aq.T, grad_bq, grad_av.T, grad_bv)
+
     mixed, grad_one, grad_q, grad_k, grad_v, far_rows, sums = middle(
-        fast,
+        False,
         lengths,
+        jnp.zeros((1, 1), jnp.float32),
         norms,
         q_own,
         k_all,
         v_all,
+        (k_all, v_all, rows_all),
         tokens,
         cotangent,
         weights,
         full,
         rows_all,
         ups_full,
-        (down_q_t, down_v_t),
+        downs_t,
     )
-    if fast:
-        operands = (grad_q, grad_k, grad_v, far_rows, weights, grad_one, sums)
-        grad_tokens, sums = lax.cond(
-            fewest[0, 0] >= rows_all.shape[0] // 2,
-            functools.partial(final_sums, False),
-            functools.partial(final_sums, True),
-            *operands,
-        )
-        grad_tokens, grad_aq, grad_av, grad_bq, grad_bv = hand_out(grad_tokens, sums, slim)
-        return (mixed, grad_tokens, grad_aq.T, grad_bq, grad_av.T, grad_bv)
-
     grad_rows = dot_nt(grad_k, weights[1]) + dot_nt(grad_v, weights[2])
     shared = lax.psum_scatter(
         grad_rows.astype(jnp.bfloat16), "tensor", scatter_dimension=0, tiled=True

time: 138 us -> 134 us (0.971)
  Pallas kernels: 137 us -> 132 us
    pallas_call x1, Pallas kernels: 73.2 us -> 70.4 us  [gather_all(): pl.pallas_call(gather_kernel, out_shape=(jax.ShapeDtypeStruct((2,) + grid...]
where the time goes in v4:
time: 134 us
  Pallas kernels  132 us (99%)
    pallas_call x1, Pallas kernels, gather_all(): pl.pallas_call(gather_kernel, out_shape=(jax.ShapeDtypeStruct((2,) + grid...  70.4 us
    pallas_call x1, Pallas kernels, middle(): pl.pallas_call(functools.partial(middle_kernel, near_only), out_shape=(ja...  44.3 us
    pallas_call x1, Pallas kernels, final_sums(): pl.pallas_call(functools.partial(final_kernel, reach), out_shape=(jax.Sha...  16.8 us

profile of v4, /device:TPU:0, one launch (start us, length us, event | category | flops | bytes accessed | tf_op | source)
XLA Modules:
  0.0 133.9 jit_solution(12255834428453476394)
XLA Ops:
  0.6 70.4 %gather_all.1 = (bf16[2,2,2,4,2,96,768]{6,5,4,3,2,1,0:T(8,128)(2,1)}, bf16[4,768,768]{2,1,0:T(8,128)(2,1)}, bf16[2048,768]{1,0:T(8,128)(2,1)}, bf16[512,768]{1,0...) custom-call(bf16[96,192]{1,0:T(8,128)(2,1)} %wq_ref.1, ...), custom_call_target="tpu_custom_call" | custom-call | tf_op jit(solution)/shard_map/gather_all/pallas_call | solution.py:671
  71.7 0.2 conditional.2
  71.9 44.3 %middle.1 = (bf16[512,768]{1,0:T(8,128)(2,1)}, f32[512,768]{1,0:T(8,128)}, bf16[512,768]{1,0:T(8,128)(2,1)}, bf16[2048,768]{1,0:T(8,128)(2,1)}, bf16[2048,768]{1...) custom-call(s32[1,32]{1,0:T(1,128)} %lengths_ref.3, f32[1,1]{1,0:T(1,128)} %get-tuple-element.79.fewest_ref, ...), custom_call_target="tpu_custom_call" | custom-call | tf_op jit(solution)/shard_map/middle/pallas_call | solution.py:1144
  116.2 16.8 %conditional.3 = ((bf16[512,768]{1,0:T(8,128)(2,1)S(1)}, f32[32,768]{1,0:T(8,128)S(1)})) conditional(s32[]{:T(128)} %bitcast.6, (bf16[512,768]{1,0:T(8,128)(2,1)}, bf16[2048,768]{1,0:T(8,128)(2,1)}, bf16[2048,768]{1,0:T(8,128)(2,1)}, bf16[1024,768]{1,0:T(8,128)(2,1)}, bf16[4,768,768]{2,1,0:T(8,128)(2,1)}, /*index=5*/f32[512,768]{1,0:T(8,128)}, ...), branch_computations={%region_2.0_spmd, %region_3.0_spmd} | conditional | bytes 8 | solution.py:1561
  116.2 16.8 %final_sums.1 = (bf16[512,768]{1,0:T(8,128)(2,1)S(1)}, f32[32,768]{1,0:T(8,128)S(1)}) custom-call(bf16[512,768]{1,0:T(8,128)(2,1)} %get-tuple-element.41.gq_hbm, bf16[2048,768]{1,0:T(8,128)(2,1)} %get-tuple-element.42.gk_hbm, bf16[2048,768]{1,0:T(8,128)(2,1)} %get-tuple-element.43.gv_hbm, bf16[1024,768]{1,0:T(8,128)(2,1)} %get-tuple-element.44.far_hbm, ...), custom_call_target="tpu_custom_call" | custom-call | tf_op jit(solution)/shard_map/cond/branch_1_fun/final_sums/pallas_call | solution.py:1423
  133.0 1.0 hand_out.1
  (1 shorter events, 0.0 us)

commit v5 on v4

--- a/solution.py
+++ b/solution.py
@@ -235,12 +235,12 @@
 FULL_ROWS = 96
 
 FLOWS = (
-    (0, 0, "zxy", 0.0),
-    (0, 1, "zyx", 0.0),
-    (1, 0, "xzy", 12.0),
-    (1, 1, "zyx", 24.0),
-    (2, 0, "xzy", 12.0),
-    (2, 1, "yxz", 12.0),
+    (0, 0, "zyx", 0.0),
+    (0, 1, "zxy", 0.0),
+    (1, 0, "zxy", 16.0),
+    (1, 1, "xyz", 12.0),
+    (2, 0, "yzx", 12.0),
+    (2, 1, "xzy", 4.0),
 )
 OWN = (0, 0, 0)
 

time: 134 us -> 131 us (0.978)
  Pallas kernels: 132 us -> 129 us
    pallas_call x1, Pallas kernels: 70.4 us -> 67.5 us  [gather_all(): pl.pallas_call(gather_kernel, out_shape=(jax.ShapeDtypeStruct((2,) + grid...]
where the time goes in v5:
time: 131 us; the launch traced here: 130 us
  Pallas kernels  129 us (98%)
    pallas_call x1, Pallas kernels, gather_all(): pl.pallas_call(gather_kernel, out_shape=(jax.ShapeDtypeStruct((2,) + grid...  67.5 us
    pallas_call x1, Pallas kernels, middle(): pl.pallas_call(functools.partial(middle_kernel, near_only), out_shape=(ja...  44.3 us
    pallas_call x1, Pallas kernels, final_sums(): pl.pallas_call(functools.partial(final_kernel, reach), out_shape=(jax.Sha...  16.1 us

profile of v5, /device:TPU:0, one launch (start us, length us, event | category | flops | bytes accessed | tf_op | source)
XLA Modules:
  0.0 130.4 jit_solution(16808169331712423867)
XLA Ops:
  0.6 67.5 %gather_all.1 = (bf16[2,2,2,4,2,96,768]{6,5,4,3,2,1,0:T(8,128)(2,1)}, bf16[4,768,768]{2,1,0:T(8,128)(2,1)}, bf16[2048,768]{1,0:T(8,128)(2,1)}, bf16[512,768]{1,0...) custom-call(bf16[96,192]{1,0:T(8,128)(2,1)} %wq_ref.1, ...), custom_call_target="tpu_custom_call" | custom-call | tf_op jit(solution)/shard_map/gather_all/pallas_call | solution.py:671
  68.8 0.2 conditional.2
  69.0 44.3 %middle.1 = (bf16[512,768]{1,0:T(8,128)(2,1)}, f32[512,768]{1,0:T(8,128)}, bf16[512,768]{1,0:T(8,128)(2,1)}, bf16[2048,768]{1,0:T(8,128)(2,1)}, bf16[2048,768]{1...) custom-call(s32[1,32]{1,0:T(1,128)} %lengths_ref.3, f32[1,1]{1,0:T(1,128)} %get-tuple-element.79.fewest_ref, ...), custom_call_target="tpu_custom_call" | custom-call | tf_op jit(solution)/shard_map/middle/pallas_call | solution.py:1144
  113.3 16.2 %conditional.3 = ((bf16[512,768]{1,0:T(8,128)(2,1)S(1)}, f32[32,768]{1,0:T(8,128)S(1)})) conditional(s32[]{:T(128)} %bitcast.6, (bf16[512,768]{1,0:T(8,128)(2,1)}, bf16[2048,768]{1,0:T(8,128)(2,1)}, bf16[2048,768]{1,0:T(8,128)(2,1)}, bf16[1024,768]{1,0:T(8,128)(2,1)}, bf16[4,768,768]{2,1,0:T(8,128)(2,1)}, /*index=5*/f32[512,768]{1,0:T(8,128)}, ...), branch_computations={%region_2.0_spmd, %region_3.0_spmd} | conditional | bytes 8 | solution.py:1561
  113.3 16.1 %final_sums.1 = (bf16[512,768]{1,0:T(8,128)(2,1)S(1)}, f32[32,768]{1,0:T(8,128)S(1)}) custom-call(bf16[512,768]{1,0:T(8,128)(2,1)} %get-tuple-element.41.gq_hbm, bf16[2048,768]{1,0:T(8,128)(2,1)} %get-tuple-element.42.gk_hbm, bf16[2048,768]{1,0:T(8,128)(2,1)} %get-tuple-element.43.gv_hbm, bf16[1024,768]{1,0:T(8,128)(2,1)} %get-tuple-element.44.far_hbm, ...), custom_call_target="tpu_custom_call" | custom-call | tf_op jit(solution)/shard_map/cond/branch_1_fun/final_sums/pallas_call | solution.py:1423
  129.4 1.0 hand_out.1
  (1 shorter events, 0.0 us)

commit v6 on v5

--- a/solution.py
+++ b/solution.py
@@ -14,7 +14,7 @@
 K_BLOCK = 512
 KV_BLOCK = 256
 NORM_BLOCK = 512
-FAR_CHUNKS = 4
+FAR_CHUNKS = 2
 FORWARD_GROUP = 6
 BACKWARD_GROUP = 3
 ADAPTER_SCALE = 2.0

time: 131 us -> 131 us (level)
  no operation moved by 1% of the time
where the time goes in v6:
time: 131 us; the launch traced here: 130 us
  Pallas kernels  129 us (98%)
    pallas_call x1, Pallas kernels, gather_all(): pl.pallas_call(gather_kernel, out_shape=(jax.ShapeDtypeStruct((2,) + grid...  67.5 us
    pallas_call x1, Pallas kernels, middle(): pl.pallas_call(functools.partial(middle_kernel, near_only), out_shape=(ja...  43.5 us
    pallas_call x1, Pallas kernels, final_sums(): pl.pallas_call(functools.partial(final_kernel, reach), out_shape=(jax.Sha...  16.9 us

profile of v6, /device:TPU:0, one launch (start us, length us, event | category | flops | bytes accessed | tf_op | source)
XLA Modules:
  0.0 130.3 jit_solution(9407778575257326614)
XLA Ops:
  0.6 67.5 %gather_all.1 = (bf16[2,2,2,4,2,96,768]{6,5,4,3,2,1,0:T(8,128)(2,1)}, bf16[4,768,768]{2,1,0:T(8,128)(2,1)}, bf16[2048,768]{1,0:T(8,128)(2,1)}, bf16[512,768]{1,0...) custom-call(bf16[96,192]{1,0:T(8,128)(2,1)} %wq_ref.1, ...), custom_call_target="tpu_custom_call" | custom-call | tf_op jit(solution)/shard_map/gather_all/pallas_call | solution.py:671
  68.8 0.2 conditional.2
  69.0 43.5 %middle.1 = (bf16[512,768]{1,0:T(8,128)(2,1)}, f32[512,768]{1,0:T(8,128)}, bf16[512,768]{1,0:T(8,128)(2,1)}, bf16[2048,768]{1,0:T(8,128)(2,1)}, bf16[2048,768]{1...) custom-call(s32[1,32]{1,0:T(1,128)} %lengths_ref.3, f32[1,1]{1,0:T(1,128)} %get-tuple-element.79.fewest_ref, ...), custom_call_target="tpu_custom_call" | custom-call | tf_op jit(solution)/shard_map/middle/pallas_call | solution.py:1144
  112.4 16.9 %conditional.3 = ((bf16[512,768]{1,0:T(8,128)(2,1)S(1)}, f32[32,768]{1,0:T(8,128)S(1)})) conditional(s32[]{:T(128)} %bitcast.6, (bf16[512,768]{1,0:T(8,128)(2,1)}, bf16[2048,768]{1,0:T(8,128)(2,1)}, bf16[2048,768]{1,0:T(8,128)(2,1)}, bf16[1024,768]{1,0:T(8,128)(2,1)}, bf16[4,768,768]{2,1,0:T(8,128)(2,1)}, /*index=5*/f32[512,768]{1,0:T(8,128)}, ...), branch_computations={%region_2.0_spmd, %region_3.0_spmd} | conditional | bytes 8 | solution.py:1561
  112.5 16.9 %final_sums.1 = (bf16[512,768]{1,0:T(8,128)(2,1)S(1)}, f32[32,768]{1,0:T(8,128)S(1)}) custom-call(bf16[512,768]{1,0:T(8,128)(2,1)} %get-tuple-element.41.gq_hbm, bf16[2048,768]{1,0:T(8,128)(2,1)} %get-tuple-element.42.gk_hbm, bf16[2048,768]{1,0:T(8,128)(2,1)} %get-tuple-element.43.gv_hbm, bf16[1024,768]{1,0:T(8,128)(2,1)} %get-tuple-element.44.far_hbm, ...), custom_call_target="tpu_custom_call" | custom-call | tf_op jit(solution)/shard_map/cond/branch_1_fun/final_sums/pallas_call | solution.py:1423
  129.3 1.0 hand_out.1
  (1 shorter events, 0.0 us)
